TPU v7x, 512 devices: a whole 4x4x16 slice. The times are simulated.
512 devices in a mesh: axial: 16 (over y, x), azim: 32 (over z, core).
Axes of the slice: x: 4, y: 4, z: 16, core: 2. Of those that a mesh axis runs over, the one named last changes fastest.
Arguments:
- gas_state: float32 [4, 8192, 4096], P(None, 'axial', 'azim'), may hold values from -6 to 6
- mean_flow: float32 [8192, 4096], P('axial', 'azim'), may hold values from 0.05 to 0.5
- part_target: float32 [16384, 4, 128], P(('axial', 'azim')), may hold values from -6 to 6
- part_offset: float32 [16384, 128], P(('axial', 'azim')), may hold values from 0 to 1
- part_width: float32 [16384, 128], P(('axial', 'azim')), may hold values from 0.6 to 2
- part_rate: float32 [16384, 128], P(('axial', 'azim')), may hold values from 0.1 to 1
- cell_index: int32 [16384, 128], P(('axial', 'azim')), may hold values from 0 to 127
- dest_owner: int32 [16384, 1], P(('axial', 'azim')), may hold values from 0 to 31; in each aligned block of 32 rows (0 to 31, 32 to 63, ...) at most 2 rows name the same one
- gas_row: int32 [16384], P(('axial', 'azim')), may hold values from 0 to 511
- live_count: int32 [512], P(('axial', 'azim')), may hold values from 512 to 4096
Outputs:
- new_state: float32 [4, 8192, 4096], P(None, 'axial', 'azim')
Inputs may be any that keep to these rules, and one draw needn't show every extreme that they name: `dest_owner`: at most 2 of the 32 tiles of one surface owner name the same sector.
All inputs are finite; a program needn't handle non-finite values.
Results may differ from a plain program's by a relative error of at most 0.0001.
Values sent between devices are 32-bit elements; how exact they have to be, the bound alone decides.
No kernel may reach another device: no remote copies, remote signals or barrier semaphores. Data moves between devices by JAX's collectives and lax.ppermute only.
A program may use at most 64 MiB of HBM per device.

v0:
```python
import jax
import jax.numpy as jnp
from jax import lax
from jax.sharding import PartitionSpec as P

CAP = 2


time_step = 0.8


def with_halo(cells, sides, width, closed):
    for axis, dim in sides:
        count = lax.axis_size(axis)
        ends = count if closed else count - 1
        head = lax.slice_in_dim(cells, 0, width, axis=dim)
        tail = lax.slice_in_dim(cells, cells.shape[dim] - width, cells.shape[dim], axis=dim)
        cells = jnp.concatenate(
            [
                lax.ppermute(tail, axis, [(i, (i + 1) % count) for i in range(ends)]),
                cells,
                lax.ppermute(head, axis, [((i + 1) % count, i) for i in range(ends)]),
            ],
            axis=dim,
        )
    return cells


def build_tiles(cell_ids, offsets, widths):
    width_t = cell_ids.shape[-1]
    centre = cell_ids.astype(jnp.float32) + offsets
    cell_mid = jnp.arange(width_t).astype(jnp.float32) + 0.5
    cell_gap = cell_mid[None, None, :] - centre[:, :, None]
    weight = jnp.exp(-cell_gap * cell_gap / (2.0 * widths[:, :, None] * widths[:, :, None]))
    return weight / jnp.sum(weight, axis=2, keepdims=True)


def padded_state(section_state):
    extended = with_halo(section_state, (("axial", 1),), 1, False)
    return with_halo(extended, (("azim", 2),), 1, True)


def per_device(
    gas_state,
    mean_flow,
    part_target,
    part_offset,
    part_width,
    part_rate,
    cell_index,
    dest_owner,
    gas_row,
    live_count,
):
    sectors = lax.axis_size("azim")
    tiles_dev = cell_index.shape[0]
    width_t = cell_index.shape[1]
    slot_count = sectors * CAP
    tile_set = build_tiles(cell_index, part_offset, part_width)
    particle = jnp.arange(tiles_dev)[:, None] * width_t + jnp.arange(width_t)[None, :]
    live_rate = jnp.where(particle < live_count[0], part_rate, jnp.zeros_like(part_rate))
    sector_ids = dest_owner[:, 0]
    sector_hits = (sector_ids[:, None] == jnp.arange(sectors)[None, :]).astype(jnp.int32)
    earlier = jnp.cumsum(sector_hits, axis=0) - sector_hits
    slot_of_tile = sector_ids * CAP + jnp.sum(earlier * sector_hits, axis=1)
    slot_match = (slot_of_tile[None, :] == jnp.arange(slot_count)[:, None]).astype(jnp.int32)
    filled = jnp.sum(slot_match, axis=1).astype(jnp.float32)
    source_tile = jnp.sum(slot_match * jnp.arange(tiles_dev)[None, :], axis=1)
    send_rows = gas_row[source_tile]
    send_tiles = tile_set[source_tile]
    packed = (
        jnp.concatenate([live_rate[:, None, :], part_target], axis=1)[source_tile]
        * filled[:, None, None]
    )
    row_code = send_rows.astype(jnp.float32)[:, None]
    got_tiles, got_values, got_rows = (
        lax.all_to_all(send_tiles, "azim", split_axis=0, concat_axis=0, tiled=True),
        lax.all_to_all(packed, "azim", split_axis=0, concat_axis=0, tiled=True),
        lax.all_to_all(row_code, "azim", split_axis=0, concat_axis=0, tiled=True),
    )
    rows_here = got_rows[:, 0].astype(jnp.int32)

    def coupling(section_state):
        sampled = section_state[:, rows_here, :]
        guessed = jnp.einsum("ksc,sjc->skj", sampled, got_tiles, precision=lax.Precision.HIGHEST)
        forcing = got_values[:, :1, :] * (got_values[:, 1:, :] - guessed)
        source = jnp.einsum("skj,sjc->ksc", forcing, got_tiles, precision=lax.Precision.HIGHEST)
        return jnp.zeros_like(section_state).at[:, rows_here, :].add(source)

    def tendency(section_state):
        padded = padded_state(section_state)
        axial_diff = 0.5 * (padded[:, 2:, 1:-1] - padded[:, :-2, 1:-1])
        azim_diff = 0.5 * (padded[:, 1:-1, 2:] - padded[:, 1:-1, :-2])
        divergence = axial_diff[1] + azim_diff[2]
        waves = jnp.stack([divergence, axial_diff[3], azim_diff[3], divergence])
        change = -mean_flow[None] * axial_diff - waves
        return change + coupling(section_state)

    section_one = gas_state + time_step * tendency(gas_state)
    section_two = 0.75 * gas_state + 0.25 * (section_one + time_step * tendency(section_one))
    return gas_state / 3.0 + 2.0 / 3.0 * (section_two + time_step * tendency(section_two))


def solution(mesh):
    placed = (
        P(None, "axial", "azim"),
        P("axial", "azim"),
        P(("axial", "azim"), None, None),
        P(("axial", "azim"), None),
        P(("axial", "azim"), None),
        P(("axial", "azim"), None),
        P(("axial", "azim"), None),
        P(("axial", "azim"), None),
        P(("axial", "azim")),
        P(("axial", "azim")),
    )
    return jax.shard_map(
        per_device, mesh=mesh, in_specs=placed, out_specs=P(None, "axial", "azim"), check_vma=False
    )
```

profile of v0, /device:TPU:24, one launch (start us, length us, event | category | flops | bytes accessed | tf_op | source)
XLA Modules:
  0.0 365.3 jit_solution(7750528114629335499)
XLA Ops:
  4.0 15.5 %all-to-all-start = ((f32[32,2,1]{1,2,0:T(1,128)}), f32[32,2,1]{1,2,0:T(1,128)S(1)}, u32[]{:S(2)}, u32[]{:S(2)}) async-start(f32[32,2,1]{1,2,0:T(1,128)} %bitcast.3), calls=%async_computation | async-start | bytes 32768 | tf_op jit(solution)/shard_map/all_to_all | solution.py:79
  23.3 8.6 %all-to-all-done = f32[32,2,1]{1,2,0:T(1,128)S(1)} async-done(((f32[32,2,1]{1,2,0:T(1,128)}), f32[32,2,1]{1,2,0:T(1,128)S(1)}, u32[]{:S(2)}, u32[]{:S(2)}) %all-to-all-start) | async-done | bytes 288 | tf_op jit(solution)/shard_map/all_to_all | solution.py:79
  31.9 3.9 %all-to-all-start.2 = ((f32[64,5,128]{2,1,0:T(8,128)}), f32[64,5,128]{2,1,0:T(8,128)S(1)}, u32[]{:S(2)}, u32[]{:S(2)}) async-start(f32[64,5,128]{2,1,0:T(8,128)} %broadcast_multiply_fusion.3), calls=%async_computation.2 | async-start | bytes 524288 | tf_op jit(solution)/shard_map/all_to_all | solution.py:78
  39.3 2.8 gather_fusion.1
  42.1 16.5 %all-to-all-done.2 = f32[64,5,128]{2,1,0:T(8,128)S(1)} async-done(((f32[64,5,128]{2,1,0:T(8,128)}), f32[64,5,128]{2,1,0:T(8,128)S(1)}, u32[]{:S(2)}, u32[]{:S(2)}) %all-to-all-start.2) | async-done | bytes 163872 | tf_op jit(solution)/shard_map/all_to_all | solution.py:78
  58.6 4.9 %all-to-all-start.1 = ((f32[64,128,128]{2,1,0:T(8,128)}), f32[64,128,128]{2,1,0:T(8,128)}, u32[]{:S(2)}, u32[]{:S(2)}) async-start(f32[64,128,128]{2,1,0:T(8,128)} %gather_fusion.1), calls=%async_computation.1 | async-start | bytes 8388608 | tf_op jit(solution)/shard_map/all_to_all | solution.py:77
  64.2 3.4 collective-permute-start.1
  67.6 5.0 %collective-permute-start = (f32[4,1,128]{2,0,1:T(4,128)S(1)}, f32[4,1,128]{2,0,1:T(4,128)S(1)}, u32[]{:S(2)}, u32[]{:S(2)}) collective-permute-start(f32[4,1,128]{2,0,1:T(4,128)S(1)} %get-tuple-element.30), channel_id=1, source_target_pairs={{32,0},{64,32},{96,64},{128,96},{160,128},{192,160},{224,192},{256... | collective-permute-start | bytes 6152 | tf_op jit(solution)/shard_map/ppermute | solution.py:22
  81.0 3.0 collective-permute-start.2
  85.2 151.0 %collective-permute-done.3 = f32[4,514,1]{1,0,2:T(4,128)S(1)} collective-permute-done((f32[4,514,1]{1,0,2:T(4,128)S(1)}, f32[4,514,1]{1,0,2:T(4,128)S(1)}, u32[]{:S(2)}, u32[]{:S(2)}) %collective-permute-start.3) | collective-permute-done | bytes 8256 | tf_op jit(solution)/shard_map/ppermute | solution.py:20
  239.1 3.3 fusion.14
  244.5 3.0 all-to-all-done.1
  247.5 8.9 %fusion.6 = f32[64,4,128]{2,1,0:T(4,128)S(1)} fusion(f32[64,128,128]{2,1,0:T(8,128)} %all-to-all-done.1, f32[4,64,128]{2,1,0:T(8,128)} %bitcast.34, f32[64,5,128]{2,1,0:T(8,128)S(1)} %all-to-all-done.2, f32[64,128]{1,0:T(8,128)S(1)} %bitcast.31), kind=kOutput, calls=%fused_computation.19 | convolution fusion | flops 50397184 | bytes 4620288 | tf_op jit(solution)/shard_map/ksc,sjc->skj/dot_general | solution.py:85
  256.4 5.4 %fusion.32 = f32[64,4,128]{2,1,0:T(4,128)S(1)} fusion(f32[64,4,128]{2,1,0:T(4,128)S(1)} %fusion.6, f32[64,128,128]{2,1,0:T(8,128)} %all-to-all-done.1), kind=kOutput, calls=%fused_computation.101 | convolution fusion | flops 50331648 | bytes 4456448 | tf_op jit(solution)/shard_map/skj,sjc->ksc/dot_general | solution.py:87
  261.8 2.8 scatter_fusion
  266.8 3.4 collective-permute-start.5
  270.2 4.6 %collective-permute-start.4 = (f32[4,1,128]{2,0,1:T(4,128)S(1)}, f32[4,1,128]{2,0,1:T(4,128)S(1)}, u32[]{:S(2)}, u32[]{:S(2)}) collective-permute-start(f32[4,1,128]{2,0,1:T(4,128)S(1)} %get-tuple-element.26), channel_id=1, source_target_pairs={{32,0},{64,32},{96,64},{128,96},{160,128},{192,160},{224,192},{256... | collective-permute-start | bytes 6152 | tf_op jit(solution)/shard_map/ppermute | solution.py:22
  274.8 9.5 %fusion.5 = f32[64,4,128]{2,1,0:T(4,128)} fusion(f32[64,128,128]{2,1,0:T(8,128)} %all-to-all-done.1, f32[64,4,128]{2,1,0:T(4,128)} %gather_fusion.4, f32[64,5,128]{2,1,0:T(8,128)S(1)} %all-to-all-done.2, f32[64,128]{1,0:T(8,128)S(1)} %bitcast.32), kind=kOutput, calls=%fused_computation.17 | convolution fusion | flops 50397184 | bytes 4620288 | tf_op jit(solution)/shard_map/ksc,sjc->skj/dot_general | solution.py:85
  286.5 2.2 copy.72
  288.7 4.8 %collective-permute-start.7 = (f32[4,514,1]{1,0,2:T(4,128)}, f32[4,514,1]{1,0,2:T(4,128)}, u32[]{:S(2)}, u32[]{:S(2)}) collective-permute-start(f32[4,514,1]{1,0,2:T(4,128)} %copy.72), channel_id=1, source_target_pairs={{0,1},{1,2},{2,3},{3,4},{4,5},{5,6},{6,7},{7,8},{8,9},{9,10},{10,1... | collective-permute-start | bytes 24680 | tf_op jit(solution)/shard_map/ppermute | solution.py:20
  293.5 2.2 copy.70
  295.8 5.8 %fusion.33 = f32[64,4,128]{2,1,0:T(4,128)S(1)} fusion(f32[64,4,128]{2,1,0:T(4,128)} %fusion.5, f32[64,128,128]{2,1,0:T(8,128)} %all-to-all-done.1), kind=kOutput, calls=%fused_computation.102 | convolution fusion | flops 50331648 | bytes 4456448 | tf_op jit(solution)/shard_map/skj,sjc->ksc/dot_general | solution.py:87
  301.6 2.1 copy.73
  303.7 2.1 copy.71
  305.9 4.5 %broadcast_multiply_fusion.1 = (f32[4,512,128]{2,0,1:T(4,128)S(1)}, f32[4,512,128]{2,0,1:T(4,128)S(1)}) fusion(f32[4,512,128]{2,0,1:T(4,128)S(1)} %multiply_add_fusion.2, f32[4,1,128]{2,0,1:T(4,128)S(1)} %collective-permute-done.5, f32[4,1,128]{2,0,1:T(4,128)S(1)} %collective-permute-done.4, f32[4,514,1]{2,0,1:T(4,128)} %copy.73, f32[4,514,1]{2,0,1:T(4,128)} %copy.71), kind=kLoop, calls=%fused_computation.58 | loop fusion | flops 3145728 | bytes 3166272 | tf_op jit(solution)/shard_map/mul | solution.py:92
  312.8 2.8 scatter_fusion.1
  321.7 6.2 %collective-permute-start.8 = (f32[4,1,128]{2,0,1:T(4,128)S(1)}, f32[4,1,128]{2,0,1:T(4,128)S(1)}, u32[]{:S(2)}, u32[]{:S(2)}) collective-permute-start(f32[4,1,128]{2,0,1:T(4,128)S(1)} %get-tuple-element.21), channel_id=1, source_target_pairs={{32,0},{64,32},{96,64},{128,96},{160,128},{192,160},{224,192},{256... | collective-permute-start | bytes 6152 | tf_op jit(solution)/shard_map/ppermute | solution.py:22
  327.9 9.0 %fusion.4 = f32[64,4,128]{2,1,0:T(4,128)} fusion(f32[64,128,128]{2,1,0:T(8,128)} %all-to-all-done.1, f32[64,4,128]{2,1,0:T(4,128)S(1)} %gather_fusion.5, f32[64,5,128]{2,1,0:T(8,128)S(1)} %all-to-all-done.2, f32[64,128]{1,0:T(8,128)S(1)} %bitcast.33), kind=kOutput, calls=%fused_computation.15 | convolution fusion | flops 50397184 | bytes 4620288 | tf_op jit(solution)/shard_map/ksc,sjc->skj/dot_general | solution.py:85
  342.5 2.8 collective-permute-start.10
  345.3 5.3 %fusion.34 = f32[64,4,128]{2,1,0:T(4,128)S(1)} fusion(f32[64,4,128]{2,1,0:T(4,128)S(1)} %copy-done.13, f32[64,128,128]{2,1,0:T(8,128)} %all-to-all-done.1), kind=kOutput, calls=%fused_computation.103 | convolution fusion | flops 50331648 | bytes 4456448 | tf_op jit(solution)/shard_map/skj,sjc->ksc/dot_general | solution.py:87
  353.4 4.3 %broadcast_multiply_fusion = (f32[4,512,128]{2,0,1:T(4,128)S(1)}, f32[4,512,128]{2,0,1:T(4,128)S(1)}) fusion(f32[4,512,128]{2,0,1:T(4,128)S(1)} %copy-done.3, f32[4,1,128]{2,0,1:T(4,128)S(1)} %collective-permute-done.9, f32[4,1,128]{2,0,1:T(4,128)S(1)} %collective-permute-done.8, f32[4,514,1]{2,0,1:T(4,128)} %copy.77, f32[4,514,1]{2,0,1:T(4,128)} %copy.75), kind=kLoop, calls=%fused_computation.57 | loop fusion | flops 3145728 | bytes 3166272 | tf_op jit(solution)/shard_map/mul | solution.py:92
  359.9 2.8 scatter_fusion.2
  (113 shorter events, 51.7 us)
Async XLA Ops:
  0.0 2.5 copy-start
  0.0 23.3 %copy-start.15 = (f32[32,128]{1,0:T(8,128)S(1)}, f32[32,128]{1,0:T(8,128)}, u32[]{:S(2)}) copy-start(f32[32,128]{1,0:T(8,128)} %param.14) | copy-start | bytes 49156
  0.0 23.3 %copy-start.16 = (f32[32,128]{1,0:T(8,128)S(1)}, f32[32,128]{1,0:T(8,128)}, u32[]{:S(2)}) copy-start(f32[32,128]{1,0:T(8,128)} %param.13) | copy-start | bytes 49156
  0.0 23.3 %copy-start.17 = (s32[32,128]{1,0:T(8,128)S(1)}, s32[32,128]{1,0:T(8,128)}, u32[]{:S(2)}) copy-start(s32[32,128]{1,0:T(8,128)} %param.16) | copy-start | bytes 49156
  4.0 27.9 %all-to-all-start = ((f32[32,2,1]{1,2,0:T(1,128)}), f32[32,2,1]{1,2,0:T(1,128)S(1)}, u32[]{:S(2)}, u32[]{:S(2)}) async-start(f32[32,2,1]{1,2,0:T(1,128)} %bitcast.3), calls=%async_computation | async-start | bytes 32768 | tf_op jit(solution)/shard_map/all_to_all | solution.py:79
  31.9 26.7 %all-to-all-start.2 = ((f32[64,5,128]{2,1,0:T(8,128)}), f32[64,5,128]{2,1,0:T(8,128)S(1)}, u32[]{:S(2)}, u32[]{:S(2)}) async-start(f32[64,5,128]{2,1,0:T(8,128)} %broadcast_multiply_fusion.3), calls=%async_computation.2 | async-start | bytes 524288 | tf_op jit(solution)/shard_map/all_to_all | solution.py:78
  42.1 21.3 %copy-start.1 = (f32[4,512,128]{2,1,0:T(8,128)S(1)}, f32[4,512,128]{2,1,0:T(8,128)}, u32[]{:S(2)}) copy-start(f32[4,512,128]{2,1,0:T(8,128)} %param.10) | copy-start | bytes 3145732
  58.6 188.9 %all-to-all-start.1 = ((f32[64,128,128]{2,1,0:T(8,128)}), f32[64,128,128]{2,1,0:T(8,128)}, u32[]{:S(2)}, u32[]{:S(2)}) async-start(f32[64,128,128]{2,1,0:T(8,128)} %gather_fusion.1), calls=%async_computation.1 | async-start | bytes 8388608 | tf_op jit(solution)/shard_map/all_to_all | solution.py:77
  63.5 9.1 %copy-start.14 = (f32[512,128]{1,0:T(8,128)S(1)}, f32[512,128]{1,0:T(8,128)}, u32[]{:S(2)}) copy-start(f32[512,128]{1,0:T(8,128)} %param.11) | copy-start | bytes 786436
  64.2 10.8 %collective-permute-start.1 = (f32[4,1,128]{2,0,1:T(4,128)S(1)}, f32[4,1,128]{2,0,1:T(4,128)S(1)}, u32[]{:S(2)}, u32[]{:S(2)}) collective-permute-start(f32[4,1,128]{2,0,1:T(4,128)S(1)} %get-tuple-element.31), channel_id=1, source_target_pairs={{0,32},{32,64},{64,96},{96,128},{128,160},{160,192},{192,224},{224... | collective-permute-start | bytes 6152 | tf_op jit(solution)/shard_map/ppermute | solution.py:20
  67.6 8.1 %collective-permute-start = (f32[4,1,128]{2,0,1:T(4,128)S(1)}, f32[4,1,128]{2,0,1:T(4,128)S(1)}, u32[]{:S(2)}, u32[]{:S(2)}) collective-permute-start(f32[4,1,128]{2,0,1:T(4,128)S(1)} %get-tuple-element.30), channel_id=1, source_target_pairs={{32,0},{64,32},{96,64},{128,96},{160,128},{192,160},{224,192},{256... | collective-permute-start | bytes 6152 | tf_op jit(solution)/shard_map/ppermute | solution.py:22
  73.5 192.0 %copy-start.18 = (s32[1024]{0:T(1024)}, s32[1024]{0:T(1024)S(1)}, u32[]{:S(2)}) copy-start(s32[1024]{0:T(1024)S(1)} %pad_clamp_fusion) | copy-start | bytes 12292
  79.3 156.8 %collective-permute-start.3 = (f32[4,514,1]{1,0,2:T(4,128)S(1)}, f32[4,514,1]{1,0,2:T(4,128)S(1)}, u32[]{:S(2)}, u32[]{:S(2)}) collective-permute-start(f32[4,514,1]{1,0,2:T(4,128)S(1)} %copy.64), channel_id=1, source_target_pairs={{0,1},{1,2},{2,3},{3,4},{4,5},{5,6},{6,7},{7,8},{8,9},{9,10},{10,1... | collective-permute-start | bytes 24680 | tf_op jit(solution)/shard_map/ppermute | solution.py:20
  81.0 156.7 %collective-permute-start.2 = (f32[4,514,1]{1,0,2:T(4,128)S(1)}, f32[4,514,1]{1,0,2:T(4,128)S(1)}, u32[]{:S(2)}, u32[]{:S(2)}) collective-permute-start(f32[4,514,1]{1,0,2:T(4,128)S(1)} %copy.62), channel_id=1, source_target_pairs={{1,0},{2,1},{3,2},{4,3},{5,4},{6,5},{7,6},{8,7},{9,8},{10,9},{11,1... | collective-permute-start | bytes 24680 | tf_op jit(solution)/shard_map/ppermute | solution.py:22
  239.1 3.3 copy-start.9
  244.5 3.0 copy-start.10
  264.6 10.2 %copy-start.11 = (f32[64,1,128]{2,1,0:T(1,128)S(1)}, f32[64,1,128]{2,1,0:T(1,128)}, u32[]{:S(2)}) copy-start(f32[64,1,128]{2,1,0:T(1,128)} %copy-done.10) | copy-start | bytes 98308
  265.5 40.4 %copy-start.4 = (f32[4,512,128]{2,0,1:T(4,128)}, f32[4,512,128]{2,0,1:T(4,128)S(1)}, u32[]{:S(2)}) copy-start(f32[4,512,128]{2,0,1:T(4,128)S(1)} %multiply_add_fusion.2) | copy-start | bytes 3145732
  266.8 17.5 %collective-permute-start.5 = (f32[4,1,128]{2,0,1:T(4,128)S(1)}, f32[4,1,128]{2,0,1:T(4,128)S(1)}, u32[]{:S(2)}, u32[]{:S(2)}) collective-permute-start(f32[4,1,128]{2,0,1:T(4,128)S(1)} %get-tuple-element.25), channel_id=1, source_target_pairs={{0,32},{32,64},{64,96},{96,128},{128,160},{160,192},{192,224},{224... | collective-permute-start | bytes 6152 | tf_op jit(solution)/shard_map/ppermute | solution.py:20
  270.2 14.1 %collective-permute-start.4 = (f32[4,1,128]{2,0,1:T(4,128)S(1)}, f32[4,1,128]{2,0,1:T(4,128)S(1)}, u32[]{:S(2)}, u32[]{:S(2)}) collective-permute-start(f32[4,1,128]{2,0,1:T(4,128)S(1)} %get-tuple-element.26), channel_id=1, source_target_pairs={{32,0},{64,32},{96,64},{128,96},{160,128},{192,160},{224,192},{256... | collective-permute-start | bytes 6152 | tf_op jit(solution)/shard_map/ppermute | solution.py:22
  288.7 12.9 %collective-permute-start.7 = (f32[4,514,1]{1,0,2:T(4,128)}, f32[4,514,1]{1,0,2:T(4,128)}, u32[]{:S(2)}, u32[]{:S(2)}) collective-permute-start(f32[4,514,1]{1,0,2:T(4,128)} %copy.72), channel_id=1, source_target_pairs={{0,1},{1,2},{2,3},{3,4},{4,5},{5,6},{6,7},{7,8},{8,9},{9,10},{10,1... | collective-permute-start | bytes 24680 | tf_op jit(solution)/shard_map/ppermute | solution.py:20
  295.8 8.0 %collective-permute-start.6 = (f32[4,514,1]{1,0,2:T(4,128)}, f32[4,514,1]{1,0,2:T(4,128)}, u32[]{:S(2)}, u32[]{:S(2)}) collective-permute-start(f32[4,514,1]{1,0,2:T(4,128)} %copy.70), channel_id=1, source_target_pairs={{1,0},{2,1},{3,2},{4,3},{5,4},{6,5},{7,6},{8,7},{9,8},{10,9},{11,1... | collective-permute-start | bytes 24680 | tf_op jit(solution)/shard_map/ppermute | solution.py:22
  310.4 1.2 copy-start.5
  310.4 1.3 copy-start.7
  315.6 12.3 %copy-start.12 = (f32[64,1,128]{2,1,0:T(1,128)S(1)}, f32[64,1,128]{2,1,0:T(1,128)}, u32[]{:S(2)}) copy-start(f32[64,1,128]{2,1,0:T(1,128)} %copy-done.10) | copy-start | bytes 98308
  316.8 1.0 copy-start.2
  319.8 17.1 %collective-permute-start.9 = (f32[4,1,128]{2,0,1:T(4,128)S(1)}, f32[4,1,128]{2,0,1:T(4,128)S(1)}, u32[]{:S(2)}, u32[]{:S(2)}) collective-permute-start(f32[4,1,128]{2,0,1:T(4,128)S(1)} %get-tuple-element.20), channel_id=1, source_target_pairs={{0,32},{32,64},{64,96},{96,128},{128,160},{160,192},{192,224},{224... | collective-permute-start | bytes 6152 | tf_op jit(solution)/shard_map/ppermute | solution.py:20
  321.7 15.2 %copy-start.3 = (f32[4,512,128]{2,0,1:T(4,128)S(1)}, f32[4,512,128]{2,0,1:T(4,128)}, u32[]{:S(2)}) copy-start(f32[4,512,128]{2,0,1:T(4,128)} %copy-done.2) | copy-start | bytes 3145732
  321.7 15.1 %collective-permute-start.8 = (f32[4,1,128]{2,0,1:T(4,128)S(1)}, f32[4,1,128]{2,0,1:T(4,128)S(1)}, u32[]{:S(2)}, u32[]{:S(2)}) collective-permute-start(f32[4,1,128]{2,0,1:T(4,128)S(1)} %get-tuple-element.21), channel_id=1, source_target_pairs={{32,0},{64,32},{96,64},{128,96},{160,128},{192,160},{224,192},{256... | collective-permute-start | bytes 6152 | tf_op jit(solution)/shard_map/ppermute | solution.py:22
  338.7 6.6 %copy-start.13 = (f32[64,4,128]{2,1,0:T(4,128)S(1)}, f32[64,4,128]{2,1,0:T(4,128)}, u32[]{:S(2)}) copy-start(f32[64,4,128]{2,1,0:T(4,128)} %fusion.4) | copy-start | bytes 393220
  340.4 10.2 %collective-permute-start.11 = (f32[4,514,1]{1,0,2:T(4,128)S(1)}, f32[4,514,1]{1,0,2:T(4,128)S(1)}, u32[]{:S(2)}, u32[]{:S(2)}) collective-permute-start(f32[4,514,1]{1,0,2:T(4,128)S(1)} %copy.76), channel_id=1, source_target_pairs={{0,1},{1,2},{2,3},{3,4},{4,5},{5,6},{6,7},{7,8},{8,9},{9,10},{10,1... | collective-permute-start | bytes 24680 | tf_op jit(solution)/shard_map/ppermute | solution.py:20
  342.5 9.5 %collective-permute-start.10 = (f32[4,514,1]{1,0,2:T(4,128)S(1)}, f32[4,514,1]{1,0,2:T(4,128)S(1)}, u32[]{:S(2)}, u32[]{:S(2)}) collective-permute-start(f32[4,514,1]{1,0,2:T(4,128)S(1)} %copy.74), channel_id=1, source_target_pairs={{1,0},{2,1},{3,2},{4,3},{5,4},{6,5},{7,6},{8,7},{9,8},{10,9},{11,1... | collective-permute-start | bytes 24680 | tf_op jit(solution)/shard_map/ppermute | solution.py:22
  (2 other events, 1.9 us)
where the time goes:
time: 372 us; the launch traced here: 365 us
  waiting for transfers between devices  179 us (48%)
  starting transfers between devices  60.9 us (16%)
  matrix products  43.9 us (12%)
  other arithmetic  40.7 us (11%)
  local copies, waits for them, and re-layouts  39.3 us (11%)
    ppermute x6, waiting for transfers between devices, with_halo(): lax.ppermute(tail, axis, [(i, (i + 1) % count) for i in range(ends)])  151 us
    dot_general x3, matrix products, coupling(): jnp.einsum('ksc,sjc->skj', sampled, got_tiles, precision=lax.Precision.HI...  27.3 us
    ppermute x6, starting transfers between devices, with_halo(): lax.ppermute(head, axis, [((i + 1) % count, i) for i in range(ends)])  21.5 us
    dot_general x3, matrix products, coupling(): jnp.einsum('skj,sjc->ksc', forcing, got_tiles, precision=lax.Precision.HI...  16.6 us
    all_to_all x1, waiting for transfers between devices, per_device(): lax.all_to_all(packed, 'azim', split_axis=0, concat_axis=0, tiled=True)  16.5 us
    all_to_all x1, starting transfers between devices, per_device(): lax.all_to_all(row_code, 'azim', split_axis=0, concat_axis=0, tiled=True)  15.5 us
    ppermute x6, starting transfers between devices, with_halo(): lax.ppermute(tail, axis, [(i, (i + 1) % count) for i in range(ends)])  15.2 us
    mul x3, other arithmetic, tendency(): axial_diff = 0.5 * (padded[:, 2:, 1:-1] - padded[:, :-2, 1:-1])  10.1 us
  transfers between devices with their start and end apart: 15, of which 4 were waited for; matrix products, arithmetic and copies ran while one was open for 17% of the time, Pallas kernels for 0%

commit v1 on v0

v1 whole, which is shorter than its diff:
```python
import math

import jax
import jax.numpy as jnp
from jax import lax
from jax.experimental import pallas as pl
from jax.experimental.pallas import tpu as pltpu
from jax.sharding import PartitionSpec as P

CAP = 2
CELLS = 128
VARS = 4
TOP = 8
CHUNK = 32
VMEM_BYTES = 20 * 1024 * 1024

time_step = 0.8
quarter = 0.25 * time_step
eighth = 0.125 * time_step

f32 = jnp.float32
bf16 = jnp.bfloat16


def vmem():
    return pl.BlockSpec(memory_space=pltpu.VMEM)


def smem():
    return pl.BlockSpec(memory_space=pltpu.SMEM)


def shape(dims, dtype=f32):
    return jax.ShapeDtypeStruct(dims, dtype)


def lanes_of(rows):
    return lax.broadcasted_iota(jnp.int32, (rows, CELLS), 1)


def slots_kernel(dest, gas_row, live, target, offset, width, rate, cell, send, centre_of, factor_of, live_of, used):
    tiles = offset.shape[0]
    sectors = send.shape[0] // CAP
    send[...] = jnp.zeros(send.shape, f32)
    centre_of[...] = cell[...].astype(f32) + offset[...]
    factor_of[...] = (-0.5 / math.log(2.0)) / (width[...] * width[...])
    particle = lax.broadcasted_iota(jnp.int32, (tiles, CELLS), 0) * CELLS + lanes_of(tiles)
    live_of[...] = jnp.where(particle < live[0], rate[...], 0.0)
    for s in range(sectors):
        used[s] = 0
    for t in range(tiles):
        sector = dest[t]
        earlier = used[sector]
        used[sector] = earlier + 1
        slot = sector * CAP + earlier
        send[slot, 0:1, :] = centre_of[t : t + 1, :]
        send[slot, 1:2, :] = factor_of[t : t + 1, :]
        send[slot, 2:3, :] = live_of[t : t + 1, :]
        send[slot, 3:4, :] = jnp.full((1, CELLS), gas_row[t].astype(f32))
        send[slot, 4:8, :] = target[t]


def turned(columns):
    lane = lanes_of(CELLS)
    total = jnp.zeros((CELLS, CELLS), f32)
    for i, column in enumerate(columns):
        total = jnp.where(lane == i, column, total)
    return total.T


def edge_columns(cells, first, lane):
    blocks = (cells.shape[1] - 2 * first) // CELLS
    return [
        cells[k, first + CELLS * b : first + CELLS * (b + 1), lane : lane + 1] for k in (2, 3) for b in range(blocks)
    ]


def edges_kernel(state, flow, down, up, right, left):
    rows = state.shape[1]
    for out, r in ((up, 0), (down, rows - 1)):
        for k in range(VARS):
            out[k : k + 1, :] = state[k, r : r + 1, :]
        out[4:5, :] = flow[r : r + 1, :]
        out[5:8, :] = jnp.ones((3, CELLS), f32)
    both = turned(edge_columns(state, 0, 0) + edge_columns(state, 0, CELLS - 1))
    left[...] = both[0:8, :]
    right[...] = both[8:16, :]


def chunk_rates(cells, flow, sides, r0, left_at, right_at):
    lane = lanes_of(CHUNK)
    here = slice(TOP + r0, TOP + r0 + CHUNK)
    dx = [
        0.5 * (cells[k, TOP + r0 + 1 : TOP + r0 + CHUNK + 1, :] - cells[k, TOP + r0 - 1 : TOP + r0 + CHUNK - 1, :])
        for k in range(VARS)
    ]
    dy = []
    block, within = r0 // CELLS, r0 % CELLS
    for k in (2, 3):
        cell = cells[k, here, :]
        if sides is None:
            before, after = 0.0, 0.0
        else:
            place = 4 * (k - 2) + block
            before = sides[within : within + CHUNK, left_at + place : left_at + place + 1]
            after = sides[within : within + CHUNK, right_at + place : right_at + place + 1]
        west = jnp.where(lane == 0, before, pltpu.roll(cell, 1, 1))
        east = jnp.where(lane == CELLS - 1, after, pltpu.roll(cell, CELLS - 1, 1))
        dy.append(0.5 * (east - west))
    speed = flow[r0 : r0 + CHUNK, :]
    spread = dx[1] + dy[0]
    return [
        -speed * dx[0] - spread,
        -speed * dx[1] - dx[3],
        -speed * dx[2] - dy[1],
        -speed * dx[3] - spread,
    ]


def fill_rows(cells, top, bottom):
    rows = cells.shape[1] - 2 * TOP
    for k in range(VARS):
        cells[k, TOP - 1 : TOP, :] = top[k]
        cells[k, TOP + rows : TOP + rows + 1, :] = bottom[k]


def waves_kernel(state, flow, above, below, from_left, from_right, out, padded, sides):
    rows = state.shape[1]
    padded[:, TOP : TOP + rows, :] = state[...]
    fill_rows(padded, [above[k : k + 1, :] for k in range(VARS)], [below[k : k + 1, :] for k in range(VARS)])
    sides[...] = jnp.concatenate([from_left[...], from_right[...], jnp.zeros((CELLS - 16, CELLS), f32)], 0).T
    for r0 in range(0, rows, CHUNK):
        rates = chunk_rates(padded, flow, sides, r0, 0, 8)
        for k in range(VARS):
            out[k, TOP + r0 : TOP + r0 + CHUNK, :] = state[k, r0 : r0 + CHUNK, :] + time_step * rates[k]
    fill_rows(out, [jnp.zeros((1, CELLS), f32)] * VARS, [jnp.zeros((1, CELLS), f32)] * VARS)


def sample(cells, first, row_of, samples):
    for t in range(samples.shape[0] // 8):
        r = row_of[0, t] + first
        for k in range(VARS):
            line = cells[k, pl.ds(r, 1), :]
            samples[8 * t + k : 8 * t + k + 1, :] = line
            samples[8 * t + 4 + k : 8 * t + 5 + k, :] = line


def high_and_low(values):
    high = values.astype(bf16).astype(f32)
    low_row = lax.broadcasted_iota(jnp.int32, values.shape, 0) % 8 >= 4
    return jnp.where(low_row, values - high, high)


def add_sources(samples, weights, goals, rates, row_of, out, first, scale):
    nothing = jnp.zeros((8, CELLS), f32)
    for p in range(weights.shape[0]):
        seen = high_and_low(samples[16 * p : 16 * p + 16, :]).astype(bf16)
        guess = jnp.dot(jnp.concatenate([seen, seen], 1), weights[p], preferred_element_type=f32)
        forces = []
        for i in range(2):
            part = guess[8 * i : 8 * i + 8, CELLS * i : CELLS * (i + 1)]
            part = part + pltpu.roll(part, 4, 0)
            forces.append(high_and_low(goals[2 * p + i] - rates[2 * p + i] * part))
        forces = jnp.concatenate(
            [jnp.concatenate([forces[0], nothing], 1), jnp.concatenate([nothing, forces[1]], 1)], 0
        ).astype(bf16)
        both = lax.dot_general(forces, weights[p], (((1,), (1,)), ((), ())), preferred_element_type=f32)
        both = both[:, :CELLS] + both[:, CELLS:]
        for i in range(2):
            part = both[8 * i : 8 * i + 8, :]
            part = scale * (part + pltpu.roll(part, 4, 0))
            r = row_of[0, 2 * p + i] + first
            for k in range(VARS):
                out[k, pl.ds(r, 1), :] = out[k, pl.ds(r, 1), :] + part[k : k + 1, :]


def first_kernel(
    got, waves, state, flow, weights, goals, rates, row_list, partial, down, up, packs,
    one, samples, row_of, sem,
):
    slots = got.shape[0]
    rows = state.shape[1]
    named = jnp.where(
        lax.broadcasted_iota(jnp.int32, (slots, CELLS), 0) == lanes_of(slots), got[:, 3, :], 0.0
    )
    row_list[...] = jnp.broadcast_to(jnp.sum(named, 0, keepdims=True).astype(jnp.int32), (8, CELLS))
    copy = pltpu.make_async_copy(row_list, row_of, sem)
    copy.start()
    middle = lax.broadcasted_iota(jnp.int32, (CELLS, CELLS), 0).astype(f32) + 0.5

    def build(p, carry):
        for i in range(2):
            t = 2 * p + i
            gap = middle - got[t, 0:1, :]
            weight = jnp.exp2(gap * gap * got[t, 1:2, :])
            whole = 1.0 / jnp.sum(weight, 0, keepdims=True)
            high = weight.astype(bf16)
            weights[p, 0:CELLS, CELLS * i : CELLS * (i + 1)] = high
            weights[p, CELLS : 2 * CELLS, CELLS * i : CELLS * (i + 1)] = (weight - high.astype(f32)).astype(bf16)
            scaled = got[t, 2:3, :] * whole
            target = got[t, 4:8, :]
            goals[t] = jnp.concatenate([target, target], 0) * scaled
            rates[t] = jnp.broadcast_to(scaled * whole, (8, CELLS))
        return carry

    lax.fori_loop(0, slots // 2, build, 0)
    one[...] = waves[...]
    copy.wait()
    sample(state, 0, row_of, samples)
    add_sources(samples, weights, goals, rates, row_of, one, TOP, time_step)
    sample(one, TOP, row_of, samples)
    for r0 in range(0, rows, CHUNK):
        change = chunk_rates(one, flow, None, r0, 0, 0)
        for k in range(VARS):
            partial[k, TOP + r0 : TOP + r0 + CHUNK, :] = (
                0.75 * state[k, r0 : r0 + CHUNK, :]
                + 0.25 * one[k, TOP + r0 : TOP + r0 + CHUNK, :]
                + quarter * change[k]
            )
    fill_rows(partial, [jnp.zeros((1, CELLS), f32)] * VARS, [jnp.zeros((1, CELLS), f32)] * VARS)
    add_sources(samples, weights, goals, rates, row_of, partial, TOP, quarter)
    for out, r in ((up, 0), (down, rows - 1)):
        for k in range(VARS):
            out[k : k + 1, :] = one[k, TOP + r : TOP + r + 1, :]
            out[4 + k : 5 + k, :] = partial[k, TOP + r : TOP + r + 1, :]
    columns = []
    for lane in (0, CELLS - 1):
        columns += edge_columns(one, TOP, lane) + edge_columns(partial, TOP, lane)
    packs[...] = turned(columns)[0:32, :]


def across_rows(beside, flow_row, side):
    along = [beside[k : k + 1, :] for k in range(VARS)]
    factor = -side * eighth
    return [
        factor * (flow_row * along[0] + along[1]),
        factor * (flow_row * along[1] + along[3]),
        factor * (flow_row * along[2]),
        factor * (flow_row * along[3] + along[1]),
    ]


def columns_kernel(above, below, flow, packs, right, left):
    rows = flow.shape[0]
    last = rows // CELLS - 1
    lane = lanes_of(1)
    from_above = across_rows(above, flow[0:1, :], -1)
    from_below = across_rows(below, flow[rows - 1 : rows, :], 1)
    for out, start, at in ((left, 0, 0), (right, 16, CELLS - 1)):
        out[0:16, :] = packs[start : start + 16, :]
        for k in (2, 3):
            top, low = from_above[k], from_below[k]
            if at == 0:
                low = pltpu.roll(low, CELLS - 1, 1)
            else:
                top = pltpu.roll(top, 1, 1)
            r = 8 + 4 * (k - 2)
            out[r : r + 1, :] = out[r : r + 1, :] + jnp.where(lane == 0, top, 0.0)
            r = r + last
            out[r : r + 1, :] = out[r : r + 1, :] + jnp.where(lane == CELLS - 1, low, 0.0)
        out[16:17, :] = above[2:3, :]
        out[17:18, :] = below[2:3, :]
        out[18:19, :] = above[3:4, :]
        out[19:20, :] = below[3:4, :]
        out[20:24, :] = jnp.zeros((4, CELLS), f32)


def last_kernel(
    row_of, partial, state, flow, above, below, above_first, below_first, from_left, from_right,
    up, down, packs, weights, goals, rates, out, two, sides, samples,
):
    rows = state.shape[1]
    lane = lanes_of(1)
    own_left, own_right = packs[0:8, :], packs[16:24, :]
    halo_left = from_left[8:16, :] - eighth * jnp.concatenate([own_left[4:8, :], own_left[0:4, :]], 0)
    halo_right = from_right[8:16, :] + eighth * jnp.concatenate([own_right[4:8, :], own_right[0:4, :]], 0)
    sides[...] = jnp.concatenate(
        [from_left[0:8, :], from_right[0:8, :], halo_left, halo_right, jnp.zeros((CELLS - 32, CELLS), f32)], 0
    ).T

    def corner(west, east):
        return eighth * (
            jnp.where(lane == 0, pltpu.roll(west, 1, 1), 0.0)
            - jnp.where(lane == CELLS - 1, pltpu.roll(east, CELLS - 1, 1), 0.0)
        )

    halos = []
    for near, first, own, side, r in ((above, above_first, up, 1, 16), (below, below_first, down, -1, 17)):
        added = across_rows(own, first[4:5, :], side)
        v_term = corner(from_left[r : r + 1, :], from_right[r : r + 1, :])
        p_term = corner(from_left[r + 2 : r + 3, :], from_right[r + 2 : r + 3, :])
        turn = [v_term, 0.0, p_term, v_term]
        halos.append([first[5:6, :] * (near[4 + k : 5 + k, :] + added[k] + turn[k]) for k in range(VARS)])
    fill_rows(two, halos[0], halos[1])

    wide = lanes_of(CHUNK)
    for r0 in range(0, rows, CHUNK):
        block, within = r0 // CELLS, r0 % CELLS

        def beside(place):
            west = sides[within : within + CHUNK, place : place + 1]
            east = sides[within : within + CHUNK, 8 + place : 9 + place]
            return eighth * (jnp.where(wide == 0, west, 0.0) - jnp.where(wide == CELLS - 1, east, 0.0))

        v_term, p_term = beside(block), beside(4 + block)
        here = slice(TOP + r0, TOP + r0 + CHUNK)
        two[0, here, :] = partial[0, here, :] + v_term
        two[1, here, :] = partial[1, here, :]
        two[2, here, :] = partial[2, here, :] + p_term
        two[3, here, :] = partial[3, here, :] + v_term
    for near, r, side in ((above, 0, -1), (below, rows - 1, 1)):
        added = across_rows(near, flow[r : r + 1, :], side)
        for k in range(VARS):
            two[k, TOP + r : TOP + r + 1, :] = two[k, TOP + r : TOP + r + 1, :] + added[k]

    sample(two, TOP, row_of, samples)
    for r0 in range(0, rows, CHUNK):
        change = chunk_rates(two, flow, sides, r0, 16, 24)
        for k in range(VARS):
            out[k, r0 : r0 + CHUNK, :] = state[k, r0 : r0 + CHUNK, :] / 3.0 + (2.0 / 3.0) * (
                two[k, TOP + r0 : TOP + r0 + CHUNK, :] + time_step * change[k]
            )
    add_sources(samples, weights, goals, rates, row_of, out, 0, (2.0 / 3.0) * time_step)


def to_neighbours(forward, back, axis, closed):
    count = lax.axis_size(axis)
    ends = count if closed else count - 1
    return (
        lax.ppermute(forward, axis, [(i, (i + 1) % count) for i in range(ends)]),
        lax.ppermute(back, axis, [((i + 1) % count, i) for i in range(ends)]),
    )


def per_device(
    gas_state,
    mean_flow,
    part_target,
    part_offset,
    part_width,
    part_rate,
    cell_index,
    dest_owner,
    gas_row,
    live_count,
):
    sectors = lax.axis_size("azim")
    tiles = cell_index.shape[0]
    rows = gas_state.shape[1]
    slots = sectors * CAP
    pairs = slots // 2
    padded = (VARS, rows + 2 * TOP, CELLS)
    params = pltpu.CompilerParams(vmem_limit_bytes=VMEM_BYTES)
    edge = shape((8, CELLS))

    send = pl.pallas_call(
        slots_kernel,
        out_shape=shape((slots, 8, CELLS)),
        in_specs=[smem()] * 3 + [vmem()] * 5,
        out_specs=vmem(),
        scratch_shapes=[pltpu.VMEM((tiles, CELLS), f32)] * 3 + [pltpu.SMEM((sectors,), jnp.int32)],
        name="slots",
    )(dest_owner[:, 0], gas_row, live_count, part_target, part_offset, part_width, part_rate, cell_index)
    got = lax.all_to_all(send, "azim", split_axis=0, concat_axis=0, tiled=True)

    down, up, right, left = pl.pallas_call(
        edges_kernel,
        out_shape=[edge] * 4,
        in_specs=[vmem()] * 2,
        out_specs=[vmem()] * 4,
        name="edges",
    )(gas_state, mean_flow)
    above_first, below_first = to_neighbours(down, up, "axial", False)
    from_left, from_right = to_neighbours(right, left, "azim", True)
    waves = pl.pallas_call(
        waves_kernel,
        out_shape=shape(padded),
        in_specs=[vmem()] * 6,
        out_specs=vmem(),
        scratch_shapes=[pltpu.VMEM(padded, f32), pltpu.VMEM((CELLS, CELLS), f32)],
        compiler_params=params,
        name="waves",
    )(gas_state, mean_flow, above_first, below_first, from_left, from_right)

    weights, goals, rates, row_list, partial, down, up, packs = pl.pallas_call(
        first_kernel,
        out_shape=[
            shape((pairs, 2 * CELLS, 2 * CELLS), bf16),
            shape((slots, 8, CELLS)),
            shape((slots, 8, CELLS)),
            shape((8, CELLS), jnp.int32),
            shape(padded),
            edge,
            edge,
            shape((32, CELLS)),
        ],
        in_specs=[vmem()] * 4,
        out_specs=[vmem()] * 8,
        scratch_shapes=[
            pltpu.VMEM(padded, f32),
            pltpu.VMEM((slots * 8, CELLS), f32),
            pltpu.SMEM((8, CELLS), jnp.int32),
            pltpu.SemaphoreType.DMA,
        ],
        compiler_params=params,
        name="first",
    )(got, waves, gas_state, mean_flow)
    above, below = to_neighbours(down, up, "axial", False)
    right, left = pl.pallas_call(
        columns_kernel,
        out_shape=[shape((24, CELLS))] * 2,
        in_specs=[vmem()] * 4,
        out_specs=[vmem()] * 2,
        name="columns",
    )(above, below, mean_flow, packs)
    from_left, from_right = to_neighbours(right, left, "azim", True)
    return pl.pallas_call(
        last_kernel,
        out_shape=shape(gas_state.shape),
        in_specs=[smem()] + [vmem()] * 15,
        out_specs=vmem(),
        scratch_shapes=[
            pltpu.VMEM(padded, f32),
            pltpu.VMEM((CELLS, CELLS), f32),
            pltpu.VMEM((slots * 8, CELLS), f32),
        ],
        compiler_params=params,
        name="last",
    )(
        row_list, partial, gas_state, mean_flow, above, below, above_first, below_first, from_left, from_right,
        up, down, packs, weights, goals, rates,
    )


def solution(mesh):
    placed = (
        P(None, "axial", "azim"),
        P("axial", "azim"),
        P(("axial", "azim"), None, None),
        P(("axial", "azim"), None),
        P(("axial", "azim"), None),
        P(("axial", "azim"), None),
        P(("axial", "azim"), None),
        P(("axial", "azim"), None),
        P(("axial", "azim")),
        P(("axial", "azim")),
    )
    return jax.shard_map(
        per_device, mesh=mesh, in_specs=placed, out_specs=P(None, "axial", "azim"), check_vma=False
    )
```

time: 372 us -> 81.7 us (0.22)
  the two profiles are of different devices: /device:TPU:24 before, /device:TPU:14 now
where the time goes in v1:
time: 81.7 us; the launch traced here: 81.1 us
  starting transfers between devices  33.1 us (41%)
  Pallas kernels  20 us (24%)
  waiting for transfers between devices  17.6 us (22%)
  local copies, waits for them, and re-layouts  9.65 us (12%)
    all_to_all x1, starting transfers between devices, per_device(): got = lax.all_to_all(send, 'azim', split_axis=0, concat_axis=0, tiled=True)  15.5 us
    ppermute x4, starting transfers between devices, to_neighbours(): lax.ppermute(back, axis, [((i + 1) % count, i) for i in range(ends)])  10.8 us
    unnamed x26, local copies, waits for them, and re-layouts  9.65 us
    all_to_all x1, waiting for transfers between devices, per_device(): got = lax.all_to_all(send, 'azim', split_axis=0, concat_axis=0, tiled=True)  8.5 us
    pallas_call x1, Pallas kernels, per_device(): pl.pallas_call(first_kernel, out_shape=[shape((pairs, 2 * CELLS, 2 * CELL...  8.39 us
    ppermute x4, waiting for transfers between devices, to_neighbours(): lax.ppermute(back, axis, [((i + 1) % count, i) for i in range(ends)])  7.53 us
    ppermute x4, starting transfers between devices, to_neighbours(): lax.ppermute(forward, axis, [(i, (i + 1) % count) for i in range(ends)])  6.76 us
    pallas_call x1, Pallas kernels, per_device(): pl.pallas_call(last_kernel, out_shape=shape(gas_state.shape), in_specs=[s...  5.03 us
  transfers between devices with their start and end apart: 9, of which 4 were waited for; matrix products, arithmetic and copies ran while one was open for 0% of the time, Pallas kernels for 4%

profile of v1, /device:TPU:14, one launch (start us, length us, event | category | flops | bytes accessed | tf_op | source)
XLA Modules:
  0.0 81.1 jit_solution(2279514625246294208)
XLA Ops:
  0.7 0.0 copy-start
  0.7 0.0 copy-start.1
  0.7 1.8 %slots.1 = f32[64,8,128]{2,1,0:T(8,128)} custom-call(s32[32]{0:T(128)} %bitcast.1, s32[32]{0:T(128)} %gas_row.1, s32[1]{0:T(128)S(6)} %copy.11.live, f32[32,4,128]{2,1,0:T(4,128)} %target.1, f32[32,128]{1,0:T(8,128)} %offset.1, f32[32,128]{1,0:T(8,128)} %width.1, f32[32,128]{1,0:T(8,128)} %rate.1, s32[32,128]{1,0:T(8,128)} %cell.1), custom_call_target="tpu_custom_call" | custom-call | tf_op jit(solution)/shard_map/slots/pallas_call | solution.py:356
  2.5 15.5 %all-to-all-start = ((f32[64,8,128]{2,1,0:T(8,128)}), f32[64,8,128]{2,1,0:T(8,128)S(1)}, u32[]{:S(2)}, u32[]{:S(2)}) async-start(f32[64,8,128]{2,1,0:T(8,128)} %slots.1), calls=%async_computation | async-start | bytes 524288 | tf_op jit(solution)/shard_map/all_to_all | solution.py:364
  18.0 2.2 %edges.1 = (f32[8,128]{1,0:T(8,128)}, f32[8,128]{1,0:T(8,128)}, f32[8,128]{1,0:T(8,128)}, f32[8,128]{1,0:T(8,128)}) custom-call(f32[4,512,128]{2,1,0:T(8,128)} %state.7, f32[512,128]{1,0:T(8,128)} %flow.9), custom_call_target="tpu_custom_call" | custom-call | tf_op jit(solution)/shard_map/edges/pallas_call | solution.py:366
  20.3 3.4 %collective-permute-start = (f32[8,128]{1,0:T(8,128)}, f32[8,128]{1,0:T(8,128)S(1)}, u32[]{:S(2)}, u32[]{:S(2)}) collective-permute-start(f32[8,128]{1,0:T(8,128)} %get-tuple-element.19), channel_id=1, source_target_pairs={{0,32},{32,64},{64,96},{96,128},{128,160},{160,192},{192,224},{224... | collective-permute-start | bytes 12296 | tf_op jit(solution)/shard_map/ppermute | solution.py:330
  23.6 2.4 %collective-permute-start.1 = (f32[8,128]{1,0:T(8,128)}, f32[8,128]{1,0:T(8,128)S(1)}, u32[]{:S(2)}, u32[]{:S(2)}) collective-permute-start(f32[8,128]{1,0:T(8,128)} %get-tuple-element.20), channel_id=1, source_target_pairs={{32,0},{64,32},{96,64},{128,96},{160,128},{192,160},{224,192},{256... | collective-permute-start | bytes 12296 | tf_op jit(solution)/shard_map/ppermute | solution.py:331
  26.1 0.0 collective-permute-start.2
  26.1 2.9 %collective-permute-start.3 = (f32[8,128]{1,0:T(8,128)}, f32[8,128]{1,0:T(8,128)S(1)}, u32[]{:S(2)}, u32[]{:S(2)}) collective-permute-start(f32[8,128]{1,0:T(8,128)} %get-tuple-element.22), channel_id=1, source_target_pairs={{1,0},{2,1},{3,2},{4,3},{5,4},{6,5},{7,6},{8,7},{9,8},{10,9},{11,1... | collective-permute-start | bytes 12296 | tf_op jit(solution)/shard_map/ppermute | solution.py:331
  29.1 0.0 collective-permute-done.above.above_first
  29.1 2.4 %collective-permute-done.1.below.below_first = f32[8,128]{1,0:T(8,128)S(1)} collective-permute-done((f32[8,128]{1,0:T(8,128)}, f32[8,128]{1,0:T(8,128)S(1)}, u32[]{:S(2)}, u32[]{:S(2)}) %collective-permute-start.1) | collective-permute-done | bytes 4128 | tf_op jit(solution)/shard_map/ppermute | solution.py:331
  31.5 0.9 %waves.1 = f32[4,528,128]{2,1,0:T(8,128)S(1)} custom-call(f32[4,512,128]{2,1,0:T(8,128)S(1)} %copy-done, f32[512,128]{1,0:T(8,128)S(1)} %copy-done.1, f32[8,128]{1,0:T(8,128)S(1)} %collective-permute-done.above.above_first, f32[8,128]{1,0:T(8,128)S(1)} %collective-permute-done.1.below.below_first, f32[8,128]{1,0:T(8,128)S(1)} %collective-permute-done.2.from_left, ...), custom_call_target="tpu_custom_call" | custom-call | tf_op jit(solution)/shard_map/waves/pallas_call | solution.py:375
  32.4 0.0 copy-start.2
  32.4 8.5 %all-to-all-done.got = f32[64,8,128]{2,1,0:T(8,128)S(1)} async-done(((f32[64,8,128]{2,1,0:T(8,128)}), f32[64,8,128]{2,1,0:T(8,128)S(1)}, u32[]{:S(2)}, u32[]{:S(2)}) %all-to-all-start) | async-done | bytes 262176 | tf_op jit(solution)/shard_map/all_to_all | solution.py:364
  40.9 8.4 %first.1 = (bf16[32,256,256]{2,1,0:T(8,128)(2,1)S(1)}, f32[64,8,128]{2,1,0:T(8,128)S(1)}, f32[64,8,128]{2,1,0:T(8,128)S(1)}, s32[8,128]{1,0:T(8,128)S(1)}, f32[4...) custom-call(f32[64,8,128]{2,1,0:T(8,128)S(1)} %all-to-all-done.got, ...), custom_call_target="tpu_custom_call" | custom-call | tf_op jit(solution)/shard_map/first/pallas_call | solution.py:385
  49.3 1.9 %copy-done.3 = bf16[32,256,256]{2,1,0:T(8,128)(2,1)} copy-done((bf16[32,256,256]{2,1,0:T(8,128)(2,1)}, bf16[32,256,256]{2,1,0:T(8,128)(2,1)S(1)}, u32[]{:S(2)}) %copy-start.3) | copy-done | bytes 4194328
  51.2 1.0 %copy-done.5 = f32[4,528,128]{2,1,0:T(8,128)} copy-done((f32[4,528,128]{2,1,0:T(8,128)}, f32[4,528,128]{2,1,0:T(8,128)S(1)}, u32[]{:S(2)}) %copy-start.5) | copy-done | bytes 1081368
  52.2 0.6 copy-done.7
  52.8 3.4 %collective-permute-start.4 = (f32[8,128]{1,0:T(8,128)S(1)}, f32[8,128]{1,0:T(8,128)S(1)}, u32[]{:S(2)}, u32[]{:S(2)}) collective-permute-start(f32[8,128]{1,0:T(8,128)S(1)} %get-tuple-element.25.down), channel_id=1, source_target_pairs={{0,32},{32,64},{64,96},{96,128},{128,160},{160,192},{192,224},{224... | collective-permute-start | bytes 12296 | tf_op jit(solution)/shard_map/ppermute | solution.py:330
  56.2 2.5 %collective-permute-start.5 = (f32[8,128]{1,0:T(8,128)S(1)}, f32[8,128]{1,0:T(8,128)S(1)}, u32[]{:S(2)}, u32[]{:S(2)}) collective-permute-start(f32[8,128]{1,0:T(8,128)S(1)} %get-tuple-element.26.up), channel_id=1, source_target_pairs={{32,0},{64,32},{96,64},{128,96},{160,128},{192,160},{224,192},{256... | collective-permute-start | bytes 12296 | tf_op jit(solution)/shard_map/ppermute | solution.py:331
  58.7 5.1 %collective-permute-done.5.below = f32[8,128]{1,0:T(8,128)S(1)} collective-permute-done((f32[8,128]{1,0:T(8,128)S(1)}, f32[8,128]{1,0:T(8,128)S(1)}, u32[]{:S(2)}, u32[]{:S(2)}) %collective-permute-start.5) | collective-permute-done | bytes 4128 | tf_op jit(solution)/shard_map/ppermute | solution.py:331
  63.8 0.6 copy-done.11
  64.4 1.6 %columns.1 = (f32[24,128]{1,0:T(8,128)}, f32[24,128]{1,0:T(8,128)}) custom-call(f32[8,128]{1,0:T(8,128)} %copy-done.9, f32[8,128]{1,0:T(8,128)} %copy-done.11, f32[512,128]{1,0:T(8,128)} %flow.9, f32[32,128]{1,0:T(8,128)} %copy-done.7), custom_call_target="tpu_custom_call" | custom-call | tf_op jit(solution)/shard_map/columns/pallas_call | solution.py:409
  66.0 3.0 %collective-permute-start.7 = (f32[24,128]{1,0:T(8,128)}, f32[24,128]{1,0:T(8,128)S(1)}, u32[]{:S(2)}, u32[]{:S(2)}) collective-permute-start(f32[24,128]{1,0:T(8,128)} %get-tuple-element.29), channel_id=1, source_target_pairs={{1,0},{2,1},{3,2},{4,3},{5,4},{6,5},{7,6},{8,7},{9,8},{10,9},{11,1... | collective-permute-start | bytes 36872 | tf_op jit(solution)/shard_map/ppermute | solution.py:331
  69.0 1.6 %collective-permute-done.6.from_left = f32[24,128]{1,0:T(8,128)S(1)} collective-permute-done((f32[24,128]{1,0:T(8,128)}, f32[24,128]{1,0:T(8,128)S(1)}, u32[]{:S(2)}, u32[]{:S(2)}) %collective-permute-start.6) | collective-permute-done | bytes 12320 | tf_op jit(solution)/shard_map/ppermute | solution.py:330
  70.6 0.0 collective-permute-done.7.from_right
  70.6 2.2 %copy-done.4 = bf16[32,256,256]{2,1,0:T(8,128)(2,1)S(1)} copy-done((bf16[32,256,256]{2,1,0:T(8,128)(2,1)S(1)}, bf16[32,256,256]{2,1,0:T(8,128)(2,1)}, u32[]{:S(2)}) %copy-start.4) | copy-done | bytes 4194328
  72.8 1.2 %copy-done.6 = f32[4,528,128]{2,1,0:T(8,128)S(1)} copy-done((f32[4,528,128]{2,1,0:T(8,128)S(1)}, f32[4,528,128]{2,1,0:T(8,128)}, u32[]{:S(2)}) %copy-start.6) | copy-done | bytes 1081368
  74.0 0.7 copy-done.8
  74.8 0.7 copy-done.10
  75.4 0.7 copy-done.12
  76.1 5.0 %last.1 = f32[4,512,128]{2,1,0:T(8,128)} custom-call(s32[8,128]{1,0:T(8,128)S(1)} %get-tuple-element.23.row_of, f32[4,528,128]{2,1,0:T(8,128)S(1)} %copy-done.6, f32[4,512,128]{2,1,0:T(8,128)S(1)} %copy-done, f32[512,128]{1,0:T(8,128)S(1)} %copy-done.2, f32[8,128]{1,0:T(8,128)S(1)} %copy-done.10, f32[8,128]{1,0:T(8,128)S(1)} %copy-done.12, ...), custom_call_target="tpu_custom_call" | custom-call | tf_op jit(solution)/shard_map/last/pallas_call | solution.py:417
  (18 shorter events, 0.0 us)
Async XLA Ops:
  0.7 30.8 %copy-start = (f32[4,512,128]{2,1,0:T(8,128)S(1)}, f32[4,512,128]{2,1,0:T(8,128)}, u32[]{:S(2)}) copy-start(f32[4,512,128]{2,1,0:T(8,128)} %state.7) | copy-start | bytes 3145732
  0.7 30.8 %copy-start.1 = (f32[512,128]{1,0:T(8,128)S(1)}, f32[512,128]{1,0:T(8,128)}, u32[]{:S(2)}) copy-start(f32[512,128]{1,0:T(8,128)} %flow.9) | copy-start | bytes 786436
  2.5 38.4 %all-to-all-start = ((f32[64,8,128]{2,1,0:T(8,128)}), f32[64,8,128]{2,1,0:T(8,128)S(1)}, u32[]{:S(2)}, u32[]{:S(2)}) async-start(f32[64,8,128]{2,1,0:T(8,128)} %slots.1), calls=%async_computation | async-start | bytes 524288 | tf_op jit(solution)/shard_map/all_to_all | solution.py:364
  20.3 8.8 %collective-permute-start = (f32[8,128]{1,0:T(8,128)}, f32[8,128]{1,0:T(8,128)S(1)}, u32[]{:S(2)}, u32[]{:S(2)}) collective-permute-start(f32[8,128]{1,0:T(8,128)} %get-tuple-element.19), channel_id=1, source_target_pairs={{0,32},{32,64},{64,96},{96,128},{128,160},{160,192},{192,224},{224... | collective-permute-start | bytes 12296 | tf_op jit(solution)/shard_map/ppermute | solution.py:330
  23.6 7.8 %collective-permute-start.1 = (f32[8,128]{1,0:T(8,128)}, f32[8,128]{1,0:T(8,128)S(1)}, u32[]{:S(2)}, u32[]{:S(2)}) collective-permute-start(f32[8,128]{1,0:T(8,128)} %get-tuple-element.20), channel_id=1, source_target_pairs={{32,0},{64,32},{96,64},{128,96},{160,128},{192,160},{224,192},{256... | collective-permute-start | bytes 12296 | tf_op jit(solution)/shard_map/ppermute | solution.py:331
  26.1 5.4 %collective-permute-start.2 = (f32[8,128]{1,0:T(8,128)}, f32[8,128]{1,0:T(8,128)S(1)}, u32[]{:S(2)}, u32[]{:S(2)}) collective-permute-start(f32[8,128]{1,0:T(8,128)} %get-tuple-element.21), channel_id=1, source_target_pairs={{0,1},{1,2},{2,3},{3,4},{4,5},{5,6},{6,7},{7,8},{8,9},{9,10},{10,1... | collective-permute-start | bytes 12296 | tf_op jit(solution)/shard_map/ppermute | solution.py:330
  26.1 5.4 %collective-permute-start.3 = (f32[8,128]{1,0:T(8,128)}, f32[8,128]{1,0:T(8,128)S(1)}, u32[]{:S(2)}, u32[]{:S(2)}) collective-permute-start(f32[8,128]{1,0:T(8,128)} %get-tuple-element.22), channel_id=1, source_target_pairs={{1,0},{2,1},{3,2},{4,3},{5,4},{6,5},{7,6},{8,7},{9,8},{10,9},{11,1... | collective-permute-start | bytes 12296 | tf_op jit(solution)/shard_map/ppermute | solution.py:331
  32.4 38.2 %copy-start.2 = (f32[512,128]{1,0:T(8,128)S(1)}, f32[512,128]{1,0:T(8,128)}, u32[]{:S(2)}) copy-start(f32[512,128]{1,0:T(8,128)} %flow.9) | copy-start | bytes 786436
  49.3 1.9 %copy-start.3 = (bf16[32,256,256]{2,1,0:T(8,128)(2,1)}, bf16[32,256,256]{2,1,0:T(8,128)(2,1)S(1)}, u32[]{:S(2)}) copy-start(bf16[32,256,256]{2,1,0:T(8,128)(2,1)S(1)} %get-tuple-element.30.weights) | copy-start | bytes 12582916
  51.2 1.0 %copy-start.5 = (f32[4,528,128]{2,1,0:T(8,128)}, f32[4,528,128]{2,1,0:T(8,128)S(1)}, u32[]{:S(2)}) copy-start(f32[4,528,128]{2,1,0:T(8,128)S(1)} %get-tuple-element.24.partial) | copy-start | bytes 3244036
  52.2 0.6 copy-start.7
  52.8 5.8 %collective-permute-start.4 = (f32[8,128]{1,0:T(8,128)S(1)}, f32[8,128]{1,0:T(8,128)S(1)}, u32[]{:S(2)}, u32[]{:S(2)}) collective-permute-start(f32[8,128]{1,0:T(8,128)S(1)} %get-tuple-element.25.down), channel_id=1, source_target_pairs={{0,32},{32,64},{64,96},{96,128},{128,160},{160,192},{192,224},{224... | collective-permute-start | bytes 12296 | tf_op jit(solution)/shard_map/ppermute | solution.py:330
  56.2 7.6 %collective-permute-start.5 = (f32[8,128]{1,0:T(8,128)S(1)}, f32[8,128]{1,0:T(8,128)S(1)}, u32[]{:S(2)}, u32[]{:S(2)}) collective-permute-start(f32[8,128]{1,0:T(8,128)S(1)} %get-tuple-element.26.up), channel_id=1, source_target_pairs={{32,0},{64,32},{96,64},{128,96},{160,128},{192,160},{224,192},{256... | collective-permute-start | bytes 12296 | tf_op jit(solution)/shard_map/ppermute | solution.py:331
  58.7 5.1 %copy-start.9 = (f32[8,128]{1,0:T(8,128)}, f32[8,128]{1,0:T(8,128)S(1)}, u32[]{:S(2)}) copy-start(f32[8,128]{1,0:T(8,128)S(1)} %collective-permute-done.4.above) | copy-start | bytes 12292
  63.8 0.6 copy-start.11
  66.0 4.5 %collective-permute-start.6 = (f32[24,128]{1,0:T(8,128)}, f32[24,128]{1,0:T(8,128)S(1)}, u32[]{:S(2)}, u32[]{:S(2)}) collective-permute-start(f32[24,128]{1,0:T(8,128)} %get-tuple-element.28), channel_id=1, source_target_pairs={{0,1},{1,2},{2,3},{3,4},{4,5},{5,6},{6,7},{7,8},{8,9},{9,10},{10,1... | collective-permute-start | bytes 36872 | tf_op jit(solution)/shard_map/ppermute | solution.py:330
  66.0 4.6 %collective-permute-start.7 = (f32[24,128]{1,0:T(8,128)}, f32[24,128]{1,0:T(8,128)S(1)}, u32[]{:S(2)}, u32[]{:S(2)}) collective-permute-start(f32[24,128]{1,0:T(8,128)} %get-tuple-element.29), channel_id=1, source_target_pairs={{1,0},{2,1},{3,2},{4,3},{5,4},{6,5},{7,6},{8,7},{9,8},{10,9},{11,1... | collective-permute-start | bytes 36872 | tf_op jit(solution)/shard_map/ppermute | solution.py:331
  70.6 2.2 %copy-start.4 = (bf16[32,256,256]{2,1,0:T(8,128)(2,1)S(1)}, bf16[32,256,256]{2,1,0:T(8,128)(2,1)}, u32[]{:S(2)}) copy-start(bf16[32,256,256]{2,1,0:T(8,128)(2,1)} %copy-done.3) | copy-start | bytes 12582916
  72.8 1.2 %copy-start.6 = (f32[4,528,128]{2,1,0:T(8,128)S(1)}, f32[4,528,128]{2,1,0:T(8,128)}, u32[]{:S(2)}) copy-start(f32[4,528,128]{2,1,0:T(8,128)} %copy-done.5) | copy-start | bytes 3244036
  74.0 0.7 copy-start.8
  74.8 0.7 copy-start.10
  75.4 0.7 copy-start.12

commit v2 on v1

--- a/solution.py
+++ b/solution.py
@@ -12,7 +12,7 @@
 VARS = 4
 TOP = 8
 CHUNK = 32
-VMEM_BYTES = 20 * 1024 * 1024
+MIB = 1024 * 1024
 
 time_step = 0.8
 quarter = 0.25 * time_step
@@ -28,6 +28,10 @@
 
 def smem():
     return pl.BlockSpec(memory_space=pltpu.SMEM)
+
+
+def room(mib):
+    return pltpu.CompilerParams(vmem_limit_bytes=mib * MIB)
 
 
 def shape(dims, dtype=f32):
@@ -75,13 +79,18 @@
     ]
 
 
-def edges_kernel(state, flow, down, up, right, left):
+def by_pair(first, second):
+    even = lax.axis_index("axial") % 2 == 0
+    return jnp.where(even, first, second), jnp.where(even, second, first)
+
+
+def edges_kernel(state, flow, near, far, right, left):
     rows = state.shape[1]
-    for out, r in ((up, 0), (down, rows - 1)):
-        for k in range(VARS):
-            out[k : k + 1, :] = state[k, r : r + 1, :]
-        out[4:5, :] = flow[r : r + 1, :]
-        out[5:8, :] = jnp.ones((3, CELLS), f32)
+    ends = []
+    for r in (0, rows - 1):
+        lines = [state[k, r : r + 1, :] for k in range(VARS)] + [flow[r : r + 1, :], jnp.ones((3, CELLS), f32)]
+        ends.append(jnp.concatenate(lines, 0))
+    near[...], far[...] = by_pair(ends[1], ends[0])
     both = turned(edge_columns(state, 0, 0) + edge_columns(state, 0, CELLS - 1))
     left[...] = both[0:8, :]
     right[...] = both[8:16, :]
@@ -124,8 +133,9 @@
         cells[k, TOP + rows : TOP + rows + 1, :] = bottom[k]
 
 
-def waves_kernel(state, flow, above, below, from_left, from_right, out, padded, sides):
+def waves_kernel(state, flow, near, far, from_left, from_right, out, padded, sides):
     rows = state.shape[1]
+    below, above = by_pair(near[...], far[...])
     padded[:, TOP : TOP + rows, :] = state[...]
     fill_rows(padded, [above[k : k + 1, :] for k in range(VARS)], [below[k : k + 1, :] for k in range(VARS)])
     sides[...] = jnp.concatenate([from_left[...], from_right[...], jnp.zeros((CELLS - 16, CELLS), f32)], 0).T
@@ -151,31 +161,53 @@
     return jnp.where(low_row, values - high, high)
 
 
+def seen_by(samples, weights, p):
+    seen = high_and_low(samples[16 * p : 16 * p + 16, :]).astype(bf16)
+    sums = jnp.dot(jnp.concatenate([seen, seen], 1), weights[p], preferred_element_type=f32)
+    parts = [sums[8 * i : 8 * i + 8, CELLS * i : CELLS * (i + 1)] for i in range(2)]
+    return [part + pltpu.roll(part, 4, 0) for part in parts]
+
+
+def add_pair(samples, weights, goals, rates, row_of, out, first, scale, p):
+    nothing = jnp.zeros((8, CELLS), f32)
+    sums = seen_by(samples, weights, p)
+    forces = [high_and_low(goals[2 * p + i] - rates[2 * p + i] * sums[i]) for i in range(2)]
+    forces = jnp.concatenate(
+        [jnp.concatenate([forces[0], nothing], 1), jnp.concatenate([nothing, forces[1]], 1)], 0
+    ).astype(bf16)
+    both = lax.dot_general(forces, weights[p], (((1,), (1,)), ((), ())), preferred_element_type=f32)
+    both = both[:, :CELLS] + both[:, CELLS:]
+    for i in range(2):
+        part = both[8 * i : 8 * i + 8, :]
+        part = scale * (part + pltpu.roll(part, 4, 0))
+        r = row_of[0, 2 * p + i] + first
+        for k in range(VARS):
+            out[k, pl.ds(r, 1), :] = out[k, pl.ds(r, 1), :] + part[k : k + 1, :]
+
+
 def add_sources(samples, weights, goals, rates, row_of, out, first, scale):
-    nothing = jnp.zeros((8, CELLS), f32)
     for p in range(weights.shape[0]):
-        seen = high_and_low(samples[16 * p : 16 * p + 16, :]).astype(bf16)
-        guess = jnp.dot(jnp.concatenate([seen, seen], 1), weights[p], preferred_element_type=f32)
-        forces = []
-        for i in range(2):
-            part = guess[8 * i : 8 * i + 8, CELLS * i : CELLS * (i + 1)]
-            part = part + pltpu.roll(part, 4, 0)
-            forces.append(high_and_low(goals[2 * p + i] - rates[2 * p + i] * part))
-        forces = jnp.concatenate(
-            [jnp.concatenate([forces[0], nothing], 1), jnp.concatenate([nothing, forces[1]], 1)], 0
-        ).astype(bf16)
-        both = lax.dot_general(forces, weights[p], (((1,), (1,)), ((), ())), preferred_element_type=f32)
-        both = both[:, :CELLS] + both[:, CELLS:]
-        for i in range(2):
-            part = both[8 * i : 8 * i + 8, :]
-            part = scale * (part + pltpu.roll(part, 4, 0))
-            r = row_of[0, 2 * p + i] + first
-            for k in range(VARS):
-                out[k, pl.ds(r, 1), :] = out[k, pl.ds(r, 1), :] + part[k : k + 1, :]
+        add_pair(samples, weights, goals, rates, row_of, out, first, scale, p)
+
+
+def build_pair(got, weights, goals, rates, p):
+    middle = lax.broadcasted_iota(jnp.int32, (CELLS, CELLS), 0).astype(f32) + 0.5
+    for i in range(2):
+        t = 2 * p + i
+        gap = middle - got[t, 0:1, :]
+        weight = jnp.exp2(gap * gap * got[t, 1:2, :])
+        whole = 1.0 / jnp.sum(weight, 0, keepdims=True)
+        high = weight.astype(bf16)
+        weights[p, 0:CELLS, CELLS * i : CELLS * (i + 1)] = high
+        weights[p, CELLS : 2 * CELLS, CELLS * i : CELLS * (i + 1)] = (weight - high.astype(f32)).astype(bf16)
+        scaled = got[t, 2:3, :] * whole
+        target = got[t, 4:8, :]
+        goals[t] = jnp.concatenate([target, target], 0) * scaled
+        rates[t] = jnp.broadcast_to(scaled * whole, (8, CELLS))
 
 
 def first_kernel(
-    got, waves, state, flow, weights, goals, rates, row_list, partial, down, up, packs,
+    got, waves, state, flow, weights, goals, rates, row_list, partial, near, far, packs,
     one, samples, row_of, sem,
 ):
     slots = got.shape[0]
@@ -186,28 +218,12 @@
     row_list[...] = jnp.broadcast_to(jnp.sum(named, 0, keepdims=True).astype(jnp.int32), (8, CELLS))
     copy = pltpu.make_async_copy(row_list, row_of, sem)
     copy.start()
-    middle = lax.broadcasted_iota(jnp.int32, (CELLS, CELLS), 0).astype(f32) + 0.5
-
-    def build(p, carry):
-        for i in range(2):
-            t = 2 * p + i
-            gap = middle - got[t, 0:1, :]
-            weight = jnp.exp2(gap * gap * got[t, 1:2, :])
-            whole = 1.0 / jnp.sum(weight, 0, keepdims=True)
-            high = weight.astype(bf16)
-            weights[p, 0:CELLS, CELLS * i : CELLS * (i + 1)] = high
-            weights[p, CELLS : 2 * CELLS, CELLS * i : CELLS * (i + 1)] = (weight - high.astype(f32)).astype(bf16)
-            scaled = got[t, 2:3, :] * whole
-            target = got[t, 4:8, :]
-            goals[t] = jnp.concatenate([target, target], 0) * scaled
-            rates[t] = jnp.broadcast_to(scaled * whole, (8, CELLS))
-        return carry
-
-    lax.fori_loop(0, slots // 2, build, 0)
     one[...] = waves[...]
     copy.wait()
     sample(state, 0, row_of, samples)
-    add_sources(samples, weights, goals, rates, row_of, one, TOP, time_step)
+    for p in range(slots // 2):
+        build_pair(got, weights, goals, rates, p)
+        add_pair(samples, weights, goals, rates, row_of, one, TOP, time_step, p)
     sample(one, TOP, row_of, samples)
     for r0 in range(0, rows, CHUNK):
         change = chunk_rates(one, flow, None, r0, 0, 0)
@@ -219,10 +235,10 @@
             )
     fill_rows(partial, [jnp.zeros((1, CELLS), f32)] * VARS, [jnp.zeros((1, CELLS), f32)] * VARS)
     add_sources(samples, weights, goals, rates, row_of, partial, TOP, quarter)
-    for out, r in ((up, 0), (down, rows - 1)):
-        for k in range(VARS):
-            out[k : k + 1, :] = one[k, TOP + r : TOP + r + 1, :]
-            out[4 + k : 5 + k, :] = partial[k, TOP + r : TOP + r + 1, :]
+    ends = []
+    for r in (TOP, TOP + rows - 1):
+        ends.append(jnp.concatenate([cells[k, r : r + 1, :] for cells in (one, partial) for k in range(VARS)], 0))
+    near[...], far[...] = by_pair(ends[1], ends[0])
     columns = []
     for lane in (0, CELLS - 1):
         columns += edge_columns(one, TOP, lane) + edge_columns(partial, TOP, lane)
@@ -240,8 +256,9 @@
     ]
 
 
-def columns_kernel(above, below, flow, packs, right, left):
+def columns_kernel(near, far, flow, packs, right, left):
     rows = flow.shape[0]
+    below, above = by_pair(near[...], far[...])
     last = rows // CELLS - 1
     lane = lanes_of(1)
     from_above = across_rows(above, flow[0:1, :], -1)
@@ -266,11 +283,14 @@
 
 
 def last_kernel(
-    row_of, partial, state, flow, above, below, above_first, below_first, from_left, from_right,
-    up, down, packs, weights, goals, rates, out, two, sides, samples,
+    row_of, partial, state, flow, near, far, near_first, far_first, from_left, from_right,
+    own_near, own_far, packs, weights, goals, rates, out, two, sides, samples,
 ):
     rows = state.shape[1]
     lane = lanes_of(1)
+    below, above = by_pair(near[...], far[...])
+    below_first, above_first = by_pair(near_first[...], far_first[...])
+    down, up = by_pair(own_near[...], own_far[...])
     own_left, own_right = packs[0:8, :], packs[16:24, :]
     halo_left = from_left[8:16, :] - eighth * jnp.concatenate([own_left[4:8, :], own_left[0:4, :]], 0)
     halo_right = from_right[8:16, :] + eighth * jnp.concatenate([own_right[4:8, :], own_right[0:4, :]], 0)
@@ -323,12 +343,20 @@
     add_sources(samples, weights, goals, rates, row_of, out, 0, (2.0 / 3.0) * time_step)
 
 
-def to_neighbours(forward, back, axis, closed):
-    count = lax.axis_size(axis)
-    ends = count if closed else count - 1
+def to_axial(near, far):
+    count = lax.axis_size("axial")
+
+    def pairs(start):
+        return [move for i in range(start, count - 1, 2) for move in ((i, i + 1), (i + 1, i))]
+
+    return lax.ppermute(near, "axial", pairs(0)), lax.ppermute(far, "axial", pairs(1))
+
+
+def to_azimuthal(right, left):
+    count = lax.axis_size("azim")
     return (
-        lax.ppermute(forward, axis, [(i, (i + 1) % count) for i in range(ends)]),
-        lax.ppermute(back, axis, [((i + 1) % count, i) for i in range(ends)]),
+        lax.ppermute(right, "azim", [(i, (i + 1) % count) for i in range(count)]),
+        lax.ppermute(left, "azim", [((i + 1) % count, i) for i in range(count)]),
     )
 
 
@@ -350,7 +378,6 @@
     slots = sectors * CAP
     pairs = slots // 2
     padded = (VARS, rows + 2 * TOP, CELLS)
-    params = pltpu.CompilerParams(vmem_limit_bytes=VMEM_BYTES)
     edge = shape((8, CELLS))
 
     send = pl.pallas_call(
@@ -363,26 +390,26 @@
     )(dest_owner[:, 0], gas_row, live_count, part_target, part_offset, part_width, part_rate, cell_index)
     got = lax.all_to_all(send, "azim", split_axis=0, concat_axis=0, tiled=True)
 
-    down, up, right, left = pl.pallas_call(
+    near, far, right, left = pl.pallas_call(
         edges_kernel,
         out_shape=[edge] * 4,
         in_specs=[vmem()] * 2,
         out_specs=[vmem()] * 4,
         name="edges",
     )(gas_state, mean_flow)
-    above_first, below_first = to_neighbours(down, up, "axial", False)
-    from_left, from_right = to_neighbours(right, left, "azim", True)
+    near_first, far_first = to_axial(near, far)
+    from_left, from_right = to_azimuthal(right, left)
     waves = pl.pallas_call(
         waves_kernel,
         out_shape=shape(padded),
         in_specs=[vmem()] * 6,
         out_specs=vmem(),
         scratch_shapes=[pltpu.VMEM(padded, f32), pltpu.VMEM((CELLS, CELLS), f32)],
-        compiler_params=params,
+        compiler_params=room(8),
         name="waves",
-    )(gas_state, mean_flow, above_first, below_first, from_left, from_right)
-
-    weights, goals, rates, row_list, partial, down, up, packs = pl.pallas_call(
+    )(gas_state, mean_flow, near_first, far_first, from_left, from_right)
+
+    weights, goals, rates, row_list, partial, own_near, own_far, packs = pl.pallas_call(
         first_kernel,
         out_shape=[
             shape((pairs, 2 * CELLS, 2 * CELLS), bf16),
@@ -402,18 +429,19 @@
             pltpu.SMEM((8, CELLS), jnp.int32),
             pltpu.SemaphoreType.DMA,
         ],
-        compiler_params=params,
+        compiler_params=room(16),
         name="first",
     )(got, waves, gas_state, mean_flow)
-    above, below = to_neighbours(down, up, "axial", False)
+    near, far = to_axial(own_near, own_far)
     right, left = pl.pallas_call(
         columns_kernel,
         out_shape=[shape((24, CELLS))] * 2,
         in_specs=[vmem()] * 4,
         out_specs=[vmem()] * 2,
+        compiler_params=room(2),
         name="columns",
-    )(above, below, mean_flow, packs)
-    from_left, from_right = to_neighbours(right, left, "azim", True)
+    )(near, far, mean_flow, packs)
+    from_left, from_right = to_azimuthal(right, left)
     return pl.pallas_call(
         last_kernel,
         out_shape=shape(gas_state.shape),
@@ -424,11 +452,11 @@
             pltpu.VMEM((CELLS, CELLS), f32),
             pltpu.VMEM((slots * 8, CELLS), f32),
         ],
-        compiler_params=params,
+        compiler_params=room(16),
         name="last",
     )(
-        row_list, partial, gas_state, mean_flow, above, below, above_first, below_first, from_left, from_right,
-        up, down, packs, weights, goals, rates,
+        row_list, partial, gas_state, mean_flow, near, far, near_first, far_first, from_left, from_right,
+        own_near, own_far, packs, weights, goals, rates,
     )
 
 

time: 81.7 us -> 68.8 us (0.84)
  the two profiles are of different devices: /device:TPU:14 before, /device:TPU:24 now
where the time goes in v2:
time: 68.8 us; the launch traced here: 68.4 us
  starting transfers between devices  36.5 us (53%)
  Pallas kernels  17.1 us (25%)
  waiting for transfers between devices  14 us (20%)
  between operations  0.74 us (1%)
    all_to_all x1, starting transfers between devices, per_device(): got = lax.all_to_all(send, 'azim', split_axis=0, concat_axis=0, tiled=True)  15.5 us
    ppermute x2, starting transfers between devices, to_axial(): lax.ppermute(far, 'axial', pairs(1))  8.36 us
    all_to_all x1, waiting for transfers between devices, per_device(): got = lax.all_to_all(send, 'azim', split_axis=0, concat_axis=0, tiled=True)  7.66 us
    pallas_call x1, Pallas kernels, per_device(): pl.pallas_call(first_kernel, out_shape=[shape((pairs, 2 * CELLS, 2 * CELL...  6.95 us
    ppermute x2, starting transfers between devices, to_axial(): lax.ppermute(near, 'axial', pairs(0))  6.78 us
    ppermute x2, starting transfers between devices, to_azimuthal(): lax.ppermute(left, 'azim', [((i + 1) % count, i) for i in range(count)])  5.9 us
    pallas_call x1, Pallas kernels, per_device(): pl.pallas_call(last_kernel, out_shape=shape(gas_state.shape), in_specs=[s...  5.1 us
    ppermute x2, waiting for transfers between devices, to_axial(): lax.ppermute(far, 'axial', pairs(1))  4.07 us
  transfers between devices with their start and end apart: 9, of which 5 were waited for; matrix products, arithmetic and copies ran while one was open for 0% of the time, Pallas kernels for 5%

profile of v2, /device:TPU:24, one launch (start us, length us, event | category | flops | bytes accessed | tf_op | source)
XLA Modules:
  0.0 68.4 jit_solution(1970421061663257128)
XLA Ops:
  0.7 0.0 copy-start
  0.7 0.0 copy-start.1
  0.7 1.8 %slots.1 = f32[64,8,128]{2,1,0:T(8,128)} custom-call(s32[32]{0:T(128)} %bitcast.1, s32[32]{0:T(128)} %gas_row.1, s32[1]{0:T(128)S(6)} %copy.11.live, f32[32,4,128]{2,1,0:T(4,128)} %target.1, f32[32,128]{1,0:T(8,128)} %offset.1, f32[32,128]{1,0:T(8,128)} %width.1, f32[32,128]{1,0:T(8,128)} %rate.1, s32[32,128]{1,0:T(8,128)} %cell.1), custom_call_target="tpu_custom_call" | custom-call | tf_op jit(solution)/shard_map/slots/pallas_call | solution.py:383
  2.5 15.5 %all-to-all-start = ((f32[64,8,128]{2,1,0:T(8,128)}), f32[64,8,128]{2,1,0:T(8,128)S(1)}, u32[]{:S(2)}, u32[]{:S(2)}) async-start(f32[64,8,128]{2,1,0:T(8,128)} %slots.1), calls=%async_computation | async-start | bytes 524288 | tf_op jit(solution)/shard_map/all_to_all | solution.py:391
  18.0 2.3 %edges.1 = (f32[8,128]{1,0:T(8,128)}, f32[8,128]{1,0:T(8,128)}, f32[8,128]{1,0:T(8,128)}, f32[8,128]{1,0:T(8,128)}) custom-call(f32[4,512,128]{2,1,0:T(8,128)} %state.7, f32[512,128]{1,0:T(8,128)} %flow.9), custom_call_target="tpu_custom_call" | custom-call | tf_op jit(solution)/shard_map/edges/pallas_call | solution.py:393
  20.3 3.4 %collective-permute-start = (f32[8,128]{1,0:T(8,128)}, f32[8,128]{1,0:T(8,128)S(1)}, u32[]{:S(2)}, u32[]{:S(2)}) collective-permute-start(f32[8,128]{1,0:T(8,128)} %get-tuple-element.19), channel_id=1, source_target_pairs={{0,32},{32,0},{64,96},{96,64},{128,160},{160,128},{192,224},{224,1... | collective-permute-start | bytes 12296 | tf_op jit(solution)/shard_map/ppermute | solution.py:352
  23.7 4.2 %collective-permute-start.1 = (f32[8,128]{1,0:T(8,128)}, f32[8,128]{1,0:T(8,128)S(1)}, u32[]{:S(2)}, u32[]{:S(2)}) collective-permute-start(f32[8,128]{1,0:T(8,128)} %get-tuple-element.20), channel_id=1, source_target_pairs={{32,64},{64,32},{96,128},{128,96},{160,192},{192,160},{224,256},{2... | collective-permute-start | bytes 12296 | tf_op jit(solution)/shard_map/ppermute | solution.py:352
  27.8 0.0 collective-permute-start.2
  27.9 2.9 %collective-permute-start.3 = (f32[8,128]{1,0:T(8,128)}, f32[8,128]{1,0:T(8,128)S(1)}, u32[]{:S(2)}, u32[]{:S(2)}) collective-permute-start(f32[8,128]{1,0:T(8,128)} %get-tuple-element.22), channel_id=1, source_target_pairs={{1,0},{2,1},{3,2},{4,3},{5,4},{6,5},{7,6},{8,7},{9,8},{10,9},{11,1... | collective-permute-start | bytes 12296 | tf_op jit(solution)/shard_map/ppermute | solution.py:359
  30.8 0.0 collective-permute-done.near.near_first
  30.8 0.7 collective-permute-done.1.far.far_first
  31.5 0.8 %collective-permute-done.2.from_left = f32[8,128]{1,0:T(8,128)S(1)} collective-permute-done((f32[8,128]{1,0:T(8,128)}, f32[8,128]{1,0:T(8,128)S(1)}, u32[]{:S(2)}, u32[]{:S(2)}) %collective-permute-start.2) | collective-permute-done | bytes 4128 | tf_op jit(solution)/shard_map/ppermute | solution.py:358
  32.3 0.0 collective-permute-done.3.from_right
  32.4 0.0 copy-done
  32.4 0.0 copy-done.1
  32.4 0.9 %waves.1 = f32[4,528,128]{2,1,0:T(8,128)S(1)} custom-call(f32[4,512,128]{2,1,0:T(8,128)S(1)} %copy-done, f32[512,128]{1,0:T(8,128)S(1)} %copy-done.1, f32[8,128]{1,0:T(8,128)S(1)} %collective-permute-done.near.near_first, f32[8,128]{1,0:T(8,128)S(1)} %collective-permute-done.1.far.far_first, f32[8,128]{1,0:T(8,128)S(1)} %collective-permute-done.2.from_left, ...), custom_call_target="tpu_custom_call" | custom-call | tf_op jit(solution)/shard_map/waves/pallas_call | solution.py:402
  33.2 7.7 %all-to-all-done.got = f32[64,8,128]{2,1,0:T(8,128)S(1)} async-done(((f32[64,8,128]{2,1,0:T(8,128)}), f32[64,8,128]{2,1,0:T(8,128)S(1)}, u32[]{:S(2)}, u32[]{:S(2)}) %all-to-all-start) | async-done | bytes 262176 | tf_op jit(solution)/shard_map/all_to_all | solution.py:391
  40.9 6.9 %first.1 = (bf16[32,256,256]{2,1,0:T(8,128)(2,1)S(1)}, f32[64,8,128]{2,1,0:T(8,128)S(1)}, f32[64,8,128]{2,1,0:T(8,128)S(1)}, s32[8,128]{1,0:T(8,128)S(1)}, f32[4...) custom-call(f32[64,8,128]{2,1,0:T(8,128)S(1)} %all-to-all-done.got, ...), custom_call_target="tpu_custom_call" | custom-call | tf_op jit(solution)/shard_map/first/pallas_call | solution.py:412
  47.8 3.4 %collective-permute-start.4 = (f32[8,128]{1,0:T(8,128)S(1)}, f32[8,128]{1,0:T(8,128)S(1)}, u32[]{:S(2)}, u32[]{:S(2)}) collective-permute-start(f32[8,128]{1,0:T(8,128)S(1)} %get-tuple-element.25.own_near), channel_id=1, source_target_pairs={{0,32},{32,0},{64,96},{96,64},{128,160},{160,128},{192,224},{224,1... | collective-permute-start | bytes 12296 | tf_op jit(solution)/shard_map/ppermute | solution.py:352
  51.2 4.2 %collective-permute-start.5 = (f32[8,128]{1,0:T(8,128)S(1)}, f32[8,128]{1,0:T(8,128)S(1)}, u32[]{:S(2)}, u32[]{:S(2)}) collective-permute-start(f32[8,128]{1,0:T(8,128)S(1)} %get-tuple-element.26.own_far), channel_id=1, source_target_pairs={{32,64},{64,32},{96,128},{128,96},{160,192},{192,160},{224,256},{2... | collective-permute-start | bytes 12296 | tf_op jit(solution)/shard_map/ppermute | solution.py:352
  55.4 0.0 collective-permute-done.4.near
  55.4 3.4 %collective-permute-done.5.far = f32[8,128]{1,0:T(8,128)S(1)} collective-permute-done((f32[8,128]{1,0:T(8,128)S(1)}, f32[8,128]{1,0:T(8,128)S(1)}, u32[]{:S(2)}, u32[]{:S(2)}) %collective-permute-start.5) | collective-permute-done | bytes 4128 | tf_op jit(solution)/shard_map/ppermute | solution.py:352
  58.9 0.1 columns.1
  58.9 0.0 collective-permute-start.6
  58.9 3.0 %collective-permute-start.7 = (f32[24,128]{1,0:T(8,128)S(1)}, f32[24,128]{1,0:T(8,128)S(1)}, u32[]{:S(2)}, u32[]{:S(2)}) collective-permute-start(f32[24,128]{1,0:T(8,128)S(1)} %get-tuple-element.29), channel_id=1, source_target_pairs={{1,0},{2,1},{3,2},{4,3},{5,4},{6,5},{7,6},{8,7},{9,8},{10,9},{11,1... | collective-permute-start | bytes 36872 | tf_op jit(solution)/shard_map/ppermute | solution.py:359
  61.9 1.4 %collective-permute-done.6.from_left = f32[24,128]{1,0:T(8,128)S(1)} collective-permute-done((f32[24,128]{1,0:T(8,128)S(1)}, f32[24,128]{1,0:T(8,128)S(1)}, u32[]{:S(2)}, u32[]{:S(2)}) %collective-permute-start.6) | collective-permute-done | bytes 12320 | tf_op jit(solution)/shard_map/ppermute | solution.py:358
  63.3 0.0 collective-permute-done.7.from_right
  63.3 5.1 %last.1 = f32[4,512,128]{2,1,0:T(8,128)} custom-call(s32[8,128]{1,0:T(8,128)S(1)} %get-tuple-element.23.row_of, f32[4,528,128]{2,1,0:T(8,128)S(1)} %get-tuple-element.24.partial, f32[4,512,128]{2,1,0:T(8,128)S(1)} %copy-done, f32[512,128]{1,0:T(8,128)S(1)} %copy-done.1, f32[8,128]{1,0:T(8,128)S(1)} %collective-permute-done.4.near, ...), custom_call_target="tpu_custom_call" | custom-call | tf_op jit(solution)/shard_map/last/pallas_call | solution.py:445
Async XLA Ops:
  0.7 31.7 %copy-start = (f32[4,512,128]{2,1,0:T(8,128)S(1)}, f32[4,512,128]{2,1,0:T(8,128)}, u32[]{:S(2)}) copy-start(f32[4,512,128]{2,1,0:T(8,128)} %state.7) | copy-start | bytes 3145732
  0.7 31.7 %copy-start.1 = (f32[512,128]{1,0:T(8,128)S(1)}, f32[512,128]{1,0:T(8,128)}, u32[]{:S(2)}) copy-start(f32[512,128]{1,0:T(8,128)} %flow.9) | copy-start | bytes 786436
  2.5 38.4 %all-to-all-start = ((f32[64,8,128]{2,1,0:T(8,128)}), f32[64,8,128]{2,1,0:T(8,128)S(1)}, u32[]{:S(2)}, u32[]{:S(2)}) async-start(f32[64,8,128]{2,1,0:T(8,128)} %slots.1), calls=%async_computation | async-start | bytes 524288 | tf_op jit(solution)/shard_map/all_to_all | solution.py:391
  20.3 10.6 %collective-permute-start = (f32[8,128]{1,0:T(8,128)}, f32[8,128]{1,0:T(8,128)S(1)}, u32[]{:S(2)}, u32[]{:S(2)}) collective-permute-start(f32[8,128]{1,0:T(8,128)} %get-tuple-element.19), channel_id=1, source_target_pairs={{0,32},{32,0},{64,96},{96,64},{128,160},{160,128},{192,224},{224,1... | collective-permute-start | bytes 12296 | tf_op jit(solution)/shard_map/ppermute | solution.py:352
  23.7 7.8 %collective-permute-start.1 = (f32[8,128]{1,0:T(8,128)}, f32[8,128]{1,0:T(8,128)S(1)}, u32[]{:S(2)}, u32[]{:S(2)}) collective-permute-start(f32[8,128]{1,0:T(8,128)} %get-tuple-element.20), channel_id=1, source_target_pairs={{32,64},{64,32},{96,128},{128,96},{160,192},{192,160},{224,256},{2... | collective-permute-start | bytes 12296 | tf_op jit(solution)/shard_map/ppermute | solution.py:352
  27.8 4.5 %collective-permute-start.2 = (f32[8,128]{1,0:T(8,128)}, f32[8,128]{1,0:T(8,128)S(1)}, u32[]{:S(2)}, u32[]{:S(2)}) collective-permute-start(f32[8,128]{1,0:T(8,128)} %get-tuple-element.21), channel_id=1, source_target_pairs={{0,1},{1,2},{2,3},{3,4},{4,5},{5,6},{6,7},{7,8},{8,9},{9,10},{10,1... | collective-permute-start | bytes 12296 | tf_op jit(solution)/shard_map/ppermute | solution.py:358
  27.9 4.5 %collective-permute-start.3 = (f32[8,128]{1,0:T(8,128)}, f32[8,128]{1,0:T(8,128)S(1)}, u32[]{:S(2)}, u32[]{:S(2)}) collective-permute-start(f32[8,128]{1,0:T(8,128)} %get-tuple-element.22), channel_id=1, source_target_pairs={{1,0},{2,1},{3,2},{4,3},{5,4},{6,5},{7,6},{8,7},{9,8},{10,9},{11,1... | collective-permute-start | bytes 12296 | tf_op jit(solution)/shard_map/ppermute | solution.py:359
  47.8 7.6 %collective-permute-start.4 = (f32[8,128]{1,0:T(8,128)S(1)}, f32[8,128]{1,0:T(8,128)S(1)}, u32[]{:S(2)}, u32[]{:S(2)}) collective-permute-start(f32[8,128]{1,0:T(8,128)S(1)} %get-tuple-element.25.own_near), channel_id=1, source_target_pairs={{0,32},{32,0},{64,96},{96,64},{128,160},{160,128},{192,224},{224,1... | collective-permute-start | bytes 12296 | tf_op jit(solution)/shard_map/ppermute | solution.py:352
  51.2 7.6 %collective-permute-start.5 = (f32[8,128]{1,0:T(8,128)S(1)}, f32[8,128]{1,0:T(8,128)S(1)}, u32[]{:S(2)}, u32[]{:S(2)}) collective-permute-start(f32[8,128]{1,0:T(8,128)S(1)} %get-tuple-element.26.own_far), channel_id=1, source_target_pairs={{32,64},{64,32},{96,128},{128,96},{160,192},{192,160},{224,256},{2... | collective-permute-start | bytes 12296 | tf_op jit(solution)/shard_map/ppermute | solution.py:352
  58.9 4.3 %collective-permute-start.6 = (f32[24,128]{1,0:T(8,128)S(1)}, f32[24,128]{1,0:T(8,128)S(1)}, u32[]{:S(2)}, u32[]{:S(2)}) collective-permute-start(f32[24,128]{1,0:T(8,128)S(1)} %get-tuple-element.28), channel_id=1, source_target_pairs={{0,1},{1,2},{2,3},{3,4},{4,5},{5,6},{6,7},{7,8},{8,9},{9,10},{10,1... | collective-permute-start | bytes 36872 | tf_op jit(solution)/shard_map/ppermute | solution.py:358
  58.9 4.4 %collective-permute-start.7 = (f32[24,128]{1,0:T(8,128)S(1)}, f32[24,128]{1,0:T(8,128)S(1)}, u32[]{:S(2)}, u32[]{:S(2)}) collective-permute-start(f32[24,128]{1,0:T(8,128)S(1)} %get-tuple-element.29), channel_id=1, source_target_pairs={{1,0},{2,1},{3,2},{4,3},{5,4},{6,5},{7,6},{8,7},{9,8},{10,9},{11,1... | collective-permute-start | bytes 36872 | tf_op jit(solution)/shard_map/ppermute | solution.py:359

commit v3 on v2

v3 whole, which is shorter than its diff:
```python
import functools
import math

import jax
import jax.numpy as jnp
from jax import lax
from jax.experimental import pallas as pl
from jax.experimental.pallas import tpu as pltpu
from jax.sharding import PartitionSpec as P

CAP = 2
CELLS = 128
VARS = 4
TOP = 8
CHUNK = 32
EACH = 7
LINES = CAP * EACH + 1
MIB = 1024 * 1024

time_step = 0.8
quarter = 0.25 * time_step
eighth = 0.125 * time_step

f32 = jnp.float32
bf16 = jnp.bfloat16


def vmem():
    return pl.BlockSpec(memory_space=pltpu.VMEM)


def smem():
    return pl.BlockSpec(memory_space=pltpu.SMEM)


def room(mib):
    return pltpu.CompilerParams(vmem_limit_bytes=mib * MIB)


def shape(dims, dtype=f32):
    return jax.ShapeDtypeStruct(dims, dtype)


def lanes_of(rows):
    return lax.broadcasted_iota(jnp.int32, (rows, CELLS), 1)


def slots_kernel(dest, gas_row, live, target, offset, width, rate, cell, send, centre_of, factor_of, live_of, latest):
    tiles = offset.shape[0]
    for t in range(tiles):
        latest[dest[t]] = t
    send[...] = jnp.zeros(send.shape, f32)
    centre_of[...] = cell[...].astype(f32) + offset[...]
    factor_of[...] = (-0.5 / math.log(2.0)) / (width[...] * width[...])
    particle = lax.broadcasted_iota(jnp.int32, (tiles, CELLS), 0) * CELLS + lanes_of(tiles)
    live_of[...] = jnp.where(particle < live[0], rate[...], 0.0)
    turn = lanes_of(1) % CAP
    for t in range(tiles):
        slot = (latest[dest[t]] == t).astype(jnp.int32)
        first = dest[t] * LINES
        at = first + slot * EACH
        send[pl.ds(at, 1), :] = centre_of[t : t + 1, :]
        send[pl.ds(at + 1, 1), :] = factor_of[t : t + 1, :]
        send[pl.ds(at + 2, 1), :] = live_of[t : t + 1, :]
        send[pl.ds(at + 3, 4), :] = target[t]
        row_line = pl.ds(first + CAP * EACH, 1)
        send[row_line, :] = jnp.where(turn == slot, gas_row[t].astype(f32), send[row_line, :])


def turned(columns):
    lane = lanes_of(CELLS)
    total = jnp.zeros((CELLS, CELLS), f32)
    for i, column in enumerate(columns):
        total = jnp.where(lane == i, column, total)
    return total.T


def edge_columns(cells, first, lane):
    height = cells.shape[0] // VARS
    starts = [k * height + first + CELLS * b for k in (2, 3) for b in range((height - 2 * first) // CELLS)]
    return [cells[at : at + CELLS, lane : lane + 1] for at in starts]


def by_pair(first, second):
    even = lax.axis_index("axial") % 2 == 0
    return jnp.where(even, first, second), jnp.where(even, second, first)


def edges_kernel(state, flow, near, far, right, left):
    rows = flow.shape[0]
    ends = []
    for r in (0, rows - 1):
        lines = [state[k * rows + r : k * rows + r + 1, :] for k in range(VARS)]
        lines += [flow[r : r + 1, :], jnp.ones((3, CELLS), f32)]
        ends.append(jnp.concatenate(lines, 0))
    near[...], far[...] = by_pair(ends[1], ends[0])
    both = turned(edge_columns(state, 0, 0) + edge_columns(state, 0, CELLS - 1))
    left[...] = both[0:8, :]
    right[...] = both[8:16, :]


def chunk_rates(cells, flow, sides, r0, left_at, right_at):
    lane = lanes_of(CHUNK)
    starts = [k * (flow.shape[0] + 2 * TOP) + TOP + r0 for k in range(VARS)]
    dx = [0.5 * (cells[at + 1 : at + CHUNK + 1, :] - cells[at - 1 : at + CHUNK - 1, :]) for at in starts]
    dy = []
    block, within = r0 // CELLS, r0 % CELLS
    for k in (2, 3):
        cell = cells[starts[k] : starts[k] + CHUNK, :]
        if sides is None:
            before, after = 0.0, 0.0
        else:
            place = 4 * (k - 2) + block
            before = sides[within : within + CHUNK, left_at + place : left_at + place + 1]
            after = sides[within : within + CHUNK, right_at + place : right_at + place + 1]
        west = jnp.where(lane == 0, before, pltpu.roll(cell, 1, 1))
        east = jnp.where(lane == CELLS - 1, after, pltpu.roll(cell, CELLS - 1, 1))
        dy.append(0.5 * (east - west))
    speed = flow[r0 : r0 + CHUNK, :]
    spread = dx[1] + dy[0]
    return [
        -speed * dx[0] - spread,
        -speed * dx[1] - dx[3],
        -speed * dx[2] - dy[1],
        -speed * dx[3] - spread,
    ]


def at_row(k, r, rows):
    return k * (rows + 2 * TOP) + TOP + r


def fill_rows(cells, top, bottom):
    height = cells.shape[0] // VARS
    for k in range(VARS):
        cells[k * height + TOP - 1 : k * height + TOP, :] = top[k]
        cells[(k + 1) * height - TOP : (k + 1) * height - TOP + 1, :] = bottom[k]


def waves_kernel(state, flow, near, far, from_left, from_right, out, padded, sides):
    rows = flow.shape[0]
    below, above = by_pair(near[...], far[...])
    for k in range(VARS):
        padded[at_row(k, 0, rows) : at_row(k, rows, rows), :] = state[k * rows : (k + 1) * rows, :]
    fill_rows(padded, [above[k : k + 1, :] for k in range(VARS)], [below[k : k + 1, :] for k in range(VARS)])
    sides[...] = jnp.concatenate([from_left[...], from_right[...], jnp.zeros((CELLS - 16, CELLS), f32)], 0).T
    for r0 in range(0, rows, CHUNK):
        rates = chunk_rates(padded, flow, sides, r0, 0, 8)
        for k in range(VARS):
            here = state[k * rows + r0 : k * rows + r0 + CHUNK, :]
            out[at_row(k, r0, rows) : at_row(k, r0 + CHUNK, rows), :] = here + time_step * rates[k]
    fill_rows(out, [jnp.zeros((1, CELLS), f32)] * VARS, [jnp.zeros((1, CELLS), f32)] * VARS)


def sample(cells, first, row_of, samples):
    for t in range(samples.shape[0] // 8):
        lines = cells[pl.ds(row_of[0, t] + first, VARS, cells.shape[0] // VARS), :]
        samples[8 * t : 8 * t + 4, :] = lines
        samples[8 * t + 4 : 8 * t + 8, :] = lines


def high_and_low(values):
    high = values.astype(bf16).astype(f32)
    low_row = lax.broadcasted_iota(jnp.int32, values.shape, 0) % 8 >= 4
    return jnp.where(low_row, values - high, high)


def see_pair(samples, weights, sums, p):
    seen = high_and_low(samples[16 * p : 16 * p + 16, :]).astype(bf16)
    both = jnp.dot(jnp.concatenate([seen, seen], 1), weights[p], preferred_element_type=f32)
    for i in range(2):
        part = both[8 * i : 8 * i + 8, CELLS * i : CELLS * (i + 1)]
        sums[2 * p + i] = part + pltpu.roll(part, 4, 0)


def add_sources(sums, turned_weights, goals, rates, row_of, out, first, scale):
    nothing = jnp.zeros((8, CELLS), f32)
    for p in range(turned_weights.shape[0]):
        forces = [high_and_low(goals[t] - rates[t] * sums[t]) for t in (2 * p, 2 * p + 1)]
        forces = jnp.concatenate(
            [jnp.concatenate([forces[0], nothing], 1), jnp.concatenate([nothing, forces[1]], 1)], 0
        ).astype(bf16)
        both = jnp.dot(forces, turned_weights[p], preferred_element_type=f32)
        both = both[:, :CELLS] + both[:, CELLS:]
        for i in range(2):
            part = both[8 * i : 8 * i + 8, :]
            part = scale * (part[0:4, :] + part[4:8, :])
            lines = pl.ds(row_of[0, 2 * p + i] + first, VARS, out.shape[0] // VARS)
            out[lines, :] = out[lines, :] + part


def build_pair(got, weights, turned_weights, goals, rates, p):
    middle = lax.broadcasted_iota(jnp.int32, (CELLS, CELLS), 0).astype(f32) + 0.5
    for i in range(2):
        t = 2 * p + i
        at = p * LINES + i * EACH
        gap = middle - got[at : at + 1, :]
        weight = jnp.exp2(gap * gap * got[at + 1 : at + 2, :])
        whole = 1.0 / jnp.sum(weight, 0, keepdims=True)
        high = weight.astype(bf16)
        low = (weight - high.astype(f32)).astype(bf16)
        here = slice(CELLS * i, CELLS * (i + 1))
        weights[p, 0:CELLS, here] = high
        weights[p, CELLS : 2 * CELLS, here] = low
        turned_weights[p, here, 0:CELLS] = high.T
        turned_weights[p, here, CELLS : 2 * CELLS] = low.T
        scaled = got[at + 2 : at + 3, :] * whole
        target = got[at + 3 : at + 7, :]
        goals[t] = jnp.concatenate([target, target], 0) * scaled
        rates[t] = jnp.broadcast_to(scaled * whole, (8, CELLS))


def first_kernel(
    got, waves, state, flow, weights, turned_weights, goals, rates, row_list, partial, near, far, right, left,
    one, samples, sums, row_of, sem,
):
    pairs = got.shape[0] // LINES
    slots = CAP * pairs
    rows = flow.shape[0]
    lines = got[pl.ds(CAP * EACH, pairs, LINES), :]
    named = jnp.where(lax.broadcasted_iota(jnp.int32, (pairs, CELLS), 0) == lanes_of(pairs) // CAP, lines, 0.0)
    row_list[...] = jnp.broadcast_to(jnp.sum(named, 0, keepdims=True).astype(jnp.int32), (8, CELLS))
    copy = pltpu.make_async_copy(row_list, row_of, sem)
    copy.start()
    one[...] = waves[...]
    ahead = slots // 8
    for p in range(ahead):
        build_pair(got, weights, turned_weights, goals, rates, p)
    copy.wait()
    sample(state, 0, row_of, samples)
    for p in range(slots // 2):
        if p + ahead < slots // 2:
            build_pair(got, weights, turned_weights, goals, rates, p + ahead)
        see_pair(samples, weights, sums, p)
    add_sources(sums, turned_weights, goals, rates, row_of, one, TOP, time_step)
    sample(one, TOP, row_of, samples)
    for p in range(slots // 2):
        see_pair(samples, weights, sums, p)
    for r0 in range(0, rows, CHUNK):
        change = chunk_rates(one, flow, None, r0, 0, 0)
        for k in range(VARS):
            here = slice(at_row(k, r0, rows), at_row(k, r0 + CHUNK, rows))
            old = state[k * rows + r0 : k * rows + r0 + CHUNK, :]
            partial[here, :] = 0.75 * old + 0.25 * one[here, :] + quarter * change[k]
    fill_rows(partial, [jnp.zeros((1, CELLS), f32)] * VARS, [jnp.zeros((1, CELLS), f32)] * VARS)
    add_sources(sums, turned_weights, goals, rates, row_of, partial, TOP, quarter)
    ends = []
    for r in (0, rows - 1):
        starts = [at_row(k, r, rows) for k in range(VARS)]
        ends.append(jnp.concatenate([cells[at : at + 1, :] for cells in (one, partial) for at in starts], 0))
    near[...], far[...] = by_pair(ends[1], ends[0])
    columns = []
    for lane in (0, CELLS - 1):
        columns += edge_columns(one, TOP, lane) + edge_columns(partial, TOP, lane)
    packs = turned(columns)
    left[...] = jnp.concatenate([packs[0:16, :], jnp.zeros((8, CELLS), f32)], 0)
    right[...] = jnp.concatenate([packs[16:32, :], jnp.zeros((8, CELLS), f32)], 0)


def across_rows(beside, flow_row, side):
    along = [beside[k : k + 1, :] for k in range(VARS)]
    factor = -side * eighth
    return [
        factor * (flow_row * along[0] + along[1]),
        factor * (flow_row * along[1] + along[3]),
        factor * (flow_row * along[2]),
        factor * (flow_row * along[3] + along[1]),
    ]


def columns_kernel(is_far, beside, flow, right_so_far, left_so_far, right, left):
    rows = flow.shape[0]
    last = rows // CELLS - 1
    lane = lanes_of(1)
    message = beside[...]
    nothing = jnp.zeros_like(message)
    below, above = by_pair(nothing, message) if is_far else by_pair(message, nothing)
    from_above = across_rows(above, flow[0:1, :], -1)
    from_below = across_rows(below, flow[rows - 1 : rows, :], 1)
    for out, before, at in ((left, left_so_far, 0), (right, right_so_far, CELLS - 1)):
        out[...] = before[...]
        for k in (2, 3):
            top, low = from_above[k], from_below[k]
            if at == 0:
                low = pltpu.roll(low, CELLS - 1, 1)
            else:
                top = pltpu.roll(top, 1, 1)
            r = 8 + 4 * (k - 2)
            out[r : r + 1, :] = out[r : r + 1, :] + jnp.where(lane == 0, top, 0.0)
            r = r + last
            out[r : r + 1, :] = out[r : r + 1, :] + jnp.where(lane == CELLS - 1, low, 0.0)
        for r, line in ((16, above[2:3, :]), (17, below[2:3, :]), (18, above[3:4, :]), (19, below[3:4, :])):
            out[r : r + 1, :] = out[r : r + 1, :] + line


def last_kernel(
    row_of, partial, state, flow, near, far, near_first, far_first, from_left, from_right,
    own_near, own_far, right, left, weights, turned_weights, goals, rates, out, two, sides, samples, sums,
):
    rows = flow.shape[0]
    lane = lanes_of(1)
    below, above = by_pair(near[...], far[...])
    below_first, above_first = by_pair(near_first[...], far_first[...])
    down, up = by_pair(own_near[...], own_far[...])
    own_left, own_right = left[0:8, :], right[0:8, :]
    halo_left = from_left[8:16, :] - eighth * jnp.concatenate([own_left[4:8, :], own_left[0:4, :]], 0)
    halo_right = from_right[8:16, :] + eighth * jnp.concatenate([own_right[4:8, :], own_right[0:4, :]], 0)
    sides[...] = jnp.concatenate(
        [from_left[0:8, :], from_right[0:8, :], halo_left, halo_right, jnp.zeros((CELLS - 32, CELLS), f32)], 0
    ).T

    def corner(west, east):
        return eighth * (
            jnp.where(lane == 0, pltpu.roll(west, 1, 1), 0.0)
            - jnp.where(lane == CELLS - 1, pltpu.roll(east, CELLS - 1, 1), 0.0)
        )

    halos = []
    for near, first, own, side, r in ((above, above_first, up, 1, 16), (below, below_first, down, -1, 17)):
        added = across_rows(own, first[4:5, :], side)
        v_term = corner(from_left[r : r + 1, :], from_right[r : r + 1, :])
        p_term = corner(from_left[r + 2 : r + 3, :], from_right[r + 2 : r + 3, :])
        turn = [v_term, 0.0, p_term, v_term]
        halos.append([first[5:6, :] * (near[4 + k : 5 + k, :] + added[k] + turn[k]) for k in range(VARS)])
    fill_rows(two, halos[0], halos[1])

    wide = lanes_of(CHUNK)
    for r0 in range(0, rows, CHUNK):
        block, within = r0 // CELLS, r0 % CELLS

        def beside(place):
            west = sides[within : within + CHUNK, place : place + 1]
            east = sides[within : within + CHUNK, 8 + place : 9 + place]
            return eighth * (jnp.where(wide == 0, west, 0.0) - jnp.where(wide == CELLS - 1, east, 0.0))

        v_term, p_term = beside(block), beside(4 + block)
        for k, term in enumerate((v_term, 0.0, p_term, v_term)):
            here = slice(at_row(k, r0, rows), at_row(k, r0 + CHUNK, rows))
            two[here, :] = partial[here, :] + term
    for near, r, side in ((above, 0, -1), (below, rows - 1, 1)):
        added = across_rows(near, flow[r : r + 1, :], side)
        for k in range(VARS):
            at = at_row(k, r, rows)
            two[at : at + 1, :] = two[at : at + 1, :] + added[k]

    sample(two, TOP, row_of, samples)
    for p in range(weights.shape[0]):
        see_pair(samples, weights, sums, p)
    for r0 in range(0, rows, CHUNK):
        change = chunk_rates(two, flow, sides, r0, 16, 24)
        for k in range(VARS):
            here = slice(k * rows + r0, k * rows + r0 + CHUNK)
            now = two[at_row(k, r0, rows) : at_row(k, r0 + CHUNK, rows), :]
            out[here, :] = state[here, :] / 3.0 + (2.0 / 3.0) * (now + time_step * change[k])
    add_sources(sums, turned_weights, goals, rates, row_of, out, 0, (2.0 / 3.0) * time_step)


def to_axial(near, far):
    count = lax.axis_size("axial")

    def pairs(start):
        return [move for i in range(start, count - 1, 2) for move in ((i, i + 1), (i + 1, i))]

    far = lax.ppermute(far, "axial", pairs(1))
    return lax.ppermute(near, "axial", pairs(0)), far


def to_azimuthal(right, left):
    count = lax.axis_size("azim")
    return (
        lax.ppermute(right, "azim", [(i, (i + 1) % count) for i in range(count)]),
        lax.ppermute(left, "azim", [((i + 1) % count, i) for i in range(count)]),
    )


def per_device(
    gas_state,
    mean_flow,
    part_target,
    part_offset,
    part_width,
    part_rate,
    cell_index,
    dest_owner,
    gas_row,
    live_count,
):
    sectors = lax.axis_size("azim")
    tiles = cell_index.shape[0]
    rows = gas_state.shape[1]
    slots = sectors * CAP
    pairs = slots // 2
    padded = (VARS * (rows + 2 * TOP), CELLS)
    state = gas_state.reshape(VARS * rows, CELLS)
    edge = shape((8, CELLS))

    send = pl.pallas_call(
        slots_kernel,
        out_shape=shape((sectors * LINES, CELLS)),
        in_specs=[smem()] * 3 + [vmem()] * 5,
        out_specs=vmem(),
        scratch_shapes=[pltpu.VMEM((tiles, CELLS), f32)] * 3 + [pltpu.SMEM((sectors,), jnp.int32)],
        name="slots",
    )(dest_owner[:, 0], gas_row, live_count, part_target, part_offset, part_width, part_rate, cell_index)
    send = send.reshape(sectors, 1, LINES * CELLS)
    got = lax.all_to_all(send, "azim", split_axis=0, concat_axis=0, tiled=True).reshape(sectors * LINES, CELLS)

    near, far, right, left = pl.pallas_call(
        edges_kernel,
        out_shape=[edge] * 4,
        in_specs=[vmem()] * 2,
        out_specs=[vmem()] * 4,
        name="edges",
    )(state, mean_flow)
    near_first, far_first = to_axial(near, far)
    from_left, from_right = to_azimuthal(right, left)
    waves = pl.pallas_call(
        waves_kernel,
        out_shape=shape(padded),
        in_specs=[vmem()] * 6,
        out_specs=vmem(),
        scratch_shapes=[pltpu.VMEM(padded, f32), pltpu.VMEM((CELLS, CELLS), f32)],
        compiler_params=room(8),
        name="waves",
    )(state, mean_flow, near_first, far_first, from_left, from_right)

    weights, turned_weights, goals, rates, row_list, partial, own_near, own_far, own_right, own_left = pl.pallas_call(
        first_kernel,
        out_shape=[
            shape((pairs, 2 * CELLS, 2 * CELLS), bf16),
            shape((pairs, 2 * CELLS, 2 * CELLS), bf16),
            shape((slots, 8, CELLS)),
            shape((slots, 8, CELLS)),
            shape((8, CELLS), jnp.int32),
            shape(padded),
            edge,
            edge,
            shape((24, CELLS)),
            shape((24, CELLS)),
        ],
        in_specs=[vmem()] * 4,
        out_specs=[vmem()] * 10,
        scratch_shapes=[
            pltpu.VMEM(padded, f32),
            pltpu.VMEM((slots * 8, CELLS), f32),
            pltpu.VMEM((slots, 8, CELLS), f32),
            pltpu.SMEM((8, CELLS), jnp.int32),
            pltpu.SemaphoreType.DMA,
        ],
        compiler_params=room(15),
        name="first",
    )(got, waves, state, mean_flow)
    near, far = to_axial(own_near, own_far)
    right, left = own_right, own_left
    for is_far, beside in ((True, far), (False, near)):
        right, left = pl.pallas_call(
            functools.partial(columns_kernel, is_far),
            out_shape=[shape((24, CELLS))] * 2,
            in_specs=[vmem()] * 4,
            out_specs=[vmem()] * 2,
            compiler_params=room(2),
            name="columns",
        )(beside, mean_flow, right, left)
    from_left, from_right = to_azimuthal(right, left)
    new_state = pl.pallas_call(
        last_kernel,
        out_shape=shape(state.shape),
        in_specs=[smem()] + [vmem()] * 17,
        out_specs=vmem(),
        scratch_shapes=[
            pltpu.VMEM(padded, f32),
            pltpu.VMEM((CELLS, CELLS), f32),
            pltpu.VMEM((slots * 8, CELLS), f32),
            pltpu.VMEM((slots, 8, CELLS), f32),
        ],
        compiler_params=room(15),
        name="last",
    )(
        row_list, partial, state, mean_flow, near, far, near_first, far_first, from_left, from_right,
        own_near, own_far, own_right, own_left, weights, turned_weights, goals, rates,
    )
    return new_state.reshape(gas_state.shape)


def solution(mesh):
    placed = (
        P(None, "axial", "azim"),
        P("axial", "azim"),
        P(("axial", "azim"), None, None),
        P(("axial", "azim"), None),
        P(("axial", "azim"), None),
        P(("axial", "azim"), None),
        P(("axial", "azim"), None),
        P(("axial", "azim"), None),
        P(("axial", "azim")),
        P(("axial", "azim")),
    )
    return jax.shard_map(
        per_device, mesh=mesh, in_specs=placed, out_specs=P(None, "axial", "azim"), check_vma=False
    )
```

time: 68.8 us -> 65.3 us (0.949)
  waiting for transfers between devices: 14 us -> 11.1 us
  Pallas kernels: 17.1 us -> 14.9 us
  local copies, waits for them, and re-layouts: 0.01 us -> 2.18 us
    all_to_all x1, waiting for transfers between devices: 7.66 us -> 4.66 us  [per_device(): lax.all_to_all(send, 'azim', split_axis=0, concat_axis=0, tiled=True)]
    unnamed x4 -> x8, local copies, waits for them, and re-layouts: 0.01 us -> 2.18 us
    pallas_call x3 -> x4, Pallas kernels: 7.03 us -> 5.82 us  [the longest x1 3.85 us: per_device(): pl.pallas_call(last_kernel, out_shape=shape(state.shape), in_specs=[smem(...]
    pallas_call x1, Pallas kernels: 6.95 us -> 5.99 us  [per_device(): pl.pallas_call(first_kernel, out_shape=[shape((pairs, 2 * CELLS, 2 * CELL...]
  transfers between devices with their start and end apart: 9 -> 9, of which waited for: 5 -> 6; matrix products, arithmetic and copies ran while one was open for 0% -> 0% of each run, Pallas kernels for 5% -> 5%
where the time goes in v3:
time: 65.3 us; the launch traced here: 64.9 us
  starting transfers between devices  35.9 us (55%)
  Pallas kernels  14.9 us (23%)
  waiting for transfers between devices  11.1 us (17%)
  local copies, waits for them, and re-layouts  2.18 us (3%)
  between operations  0.83 us (1%)
    all_to_all x1, starting transfers between devices, per_device(): lax.all_to_all(send, 'azim', split_axis=0, concat_axis=0, tiled=True)  15.5 us
    ppermute x2, starting transfers between devices, to_axial(): far = lax.ppermute(far, 'axial', pairs(1))  9.13 us
    pallas_call x1, Pallas kernels, per_device(): pl.pallas_call(first_kernel, out_shape=[shape((pairs, 2 * CELLS, 2 * CELL...  5.99 us
    ppermute x2, starting transfers between devices, to_azimuthal(): lax.ppermute(left, 'azim', [((i + 1) % count, i) for i in range(count)])  5.9 us
    ppermute x2, starting transfers between devices, to_axial(): return (lax.ppermute(near, 'axial', pairs(0)), far)  5.34 us
    all_to_all x1, waiting for transfers between devices, per_device(): lax.all_to_all(send, 'azim', split_axis=0, concat_axis=0, tiled=True)  4.66 us
    pallas_call x1, Pallas kernels, per_device(): pl.pallas_call(last_kernel, out_shape=shape(state.shape), in_specs=[smem(...  3.85 us
    ppermute x2, waiting for transfers between devices, to_axial(): return (lax.ppermute(near, 'axial', pairs(0)), far)  2.76 us
  transfers between devices with their start and end apart: 9, of which 6 were waited for; matrix products, arithmetic and copies ran while one was open for 0% of the time, Pallas kernels for 5%

profile of v3, /device:TPU:24, one launch (start us, length us, event | category | flops | bytes accessed | tf_op | source)
XLA Modules:
  0.0 64.9 jit_solution(3299115719898577032)
XLA Ops:
  0.0 0.0 copy-start.3
  0.0 0.0 copy-start.1
  0.8 1.8 %slots.1 = f32[480,128]{1,0:T(8,128)} custom-call(s32[32]{0:T(128)} %bitcast.11, s32[32]{0:T(128)} %gas_row.1, s32[1]{0:T(128)S(6)} %copy.12.live, f32[32,4,128]{2,1,0:T(4,128)} %target.1, f32[32,128]{1,0:T(8,128)} %offset.1, f32[32,128]{1,0:T(8,128)} %width.1, f32[32,128]{1,0:T(8,128)} %rate.1, s32[32,128]{1,0:T(8,128)} %cell.1), custom_call_target="tpu_custom_call" | custom-call | tf_op jit(solution)/shard_map/slots/pallas_call | solution.py:397
  2.6 15.5 %all-to-all-start = ((f32[32,1,1920]{2,1,0:T(1,128)}), f32[32,1,1920]{2,1,0:T(1,128)S(1)}, u32[]{:S(2)}, u32[]{:S(2)}) async-start(f32[32,1,1920]{2,1,0:T(1,128)} %bitcast.10), calls=%async_computation | async-start | bytes 491520 | tf_op jit(solution)/shard_map/all_to_all | solution.py:406
  18.0 2.3 %edges.1 = (f32[8,128]{1,0:T(8,128)}, f32[8,128]{1,0:T(8,128)}, f32[8,128]{1,0:T(8,128)}, f32[8,128]{1,0:T(8,128)}) custom-call(f32[2048,128]{1,0:T(8,128)} %bitcast.5, f32[512,128]{1,0:T(8,128)} %flow.11), custom_call_target="tpu_custom_call" | custom-call | tf_op jit(solution)/shard_map/edges/pallas_call | solution.py:408
  20.3 3.4 %collective-permute-start = (f32[8,128]{1,0:T(8,128)}, f32[8,128]{1,0:T(8,128)S(1)}, u32[]{:S(2)}, u32[]{:S(2)}) collective-permute-start(f32[8,128]{1,0:T(8,128)} %get-tuple-element.23), channel_id=1, source_target_pairs={{0,32},{32,0},{64,96},{96,64},{128,160},{160,128},{192,224},{224,1... | collective-permute-start | bytes 12296 | tf_op jit(solution)/shard_map/ppermute | solution.py:365
  23.7 4.2 %collective-permute-start.1 = (f32[8,128]{1,0:T(8,128)}, f32[8,128]{1,0:T(8,128)S(1)}, u32[]{:S(2)}, u32[]{:S(2)}) collective-permute-start(f32[8,128]{1,0:T(8,128)} %get-tuple-element.24), channel_id=1, source_target_pairs={{32,64},{64,32},{96,128},{128,96},{160,192},{192,160},{224,256},{2... | collective-permute-start | bytes 12296 | tf_op jit(solution)/shard_map/ppermute | solution.py:364
  27.9 0.0 collective-permute-start.2
  27.9 2.9 %collective-permute-start.3 = (f32[8,128]{1,0:T(8,128)}, f32[8,128]{1,0:T(8,128)S(1)}, u32[]{:S(2)}, u32[]{:S(2)}) collective-permute-start(f32[8,128]{1,0:T(8,128)} %get-tuple-element.26), channel_id=1, source_target_pairs={{1,0},{2,1},{3,2},{4,3},{5,4},{6,5},{7,6},{8,7},{9,8},{10,9},{11,1... | collective-permute-start | bytes 12296 | tf_op jit(solution)/shard_map/ppermute | solution.py:372
  30.9 0.0 collective-permute-done.near.near_first
  30.9 0.7 %collective-permute-done.1.far.far_first = f32[8,128]{1,0:T(8,128)S(1)} collective-permute-done((f32[8,128]{1,0:T(8,128)}, f32[8,128]{1,0:T(8,128)S(1)}, u32[]{:S(2)}, u32[]{:S(2)}) %collective-permute-start.1) | collective-permute-done | bytes 4128 | tf_op jit(solution)/shard_map/ppermute | solution.py:364
  31.5 0.9 %collective-permute-done.2.from_left = f32[8,128]{1,0:T(8,128)S(1)} collective-permute-done((f32[8,128]{1,0:T(8,128)}, f32[8,128]{1,0:T(8,128)S(1)}, u32[]{:S(2)}, u32[]{:S(2)}) %collective-permute-start.2) | collective-permute-done | bytes 4128 | tf_op jit(solution)/shard_map/ppermute | solution.py:371
  32.4 0.0 collective-permute-done.3.from_right
  32.4 0.0 copy-start
  32.4 1.2 %copy-done = f32[4,512,128]{2,1,0:T(8,128)S(1)} copy-done((f32[4,512,128]{2,1,0:T(8,128)S(1)}, f32[4,512,128]{2,1,0:T(8,128)}, u32[]{:S(2)}) %copy-start) | copy-done | bytes 1048600
  33.6 0.9 %copy-done.2 = f32[512,128]{1,0:T(8,128)S(1)} copy-done((f32[512,128]{1,0:T(8,128)S(1)}, f32[512,128]{1,0:T(8,128)}, u32[]{:S(2)}) %copy-start.2) | copy-done | bytes 262168
  34.6 0.9 %waves.1 = f32[2112,128]{1,0:T(8,128)S(1)} custom-call(f32[2048,128]{1,0:T(8,128)S(1)} %bitcast.6, f32[512,128]{1,0:T(8,128)S(1)} %copy-done.2, f32[8,128]{1,0:T(8,128)S(1)} %collective-permute-done.near.near_first, f32[8,128]{1,0:T(8,128)S(1)} %collective-permute-done.1.far.far_first, f32[8,128]{1,0:T(8,128)S(1)} %collective-permute-done.2.from_left, ...), custom_call_target="tpu_custom_call" | custom-call | tf_op jit(solution)/shard_map/waves/pallas_call | solution.py:417
  35.4 4.7 %all-to-all-done = f32[32,1,1920]{2,1,0:T(1,128)S(1)} async-done(((f32[32,1,1920]{2,1,0:T(1,128)}), f32[32,1,1920]{2,1,0:T(1,128)S(1)}, u32[]{:S(2)}, u32[]{:S(2)}) %all-to-all-start) | async-done | bytes 245792 | tf_op jit(solution)/shard_map/all_to_all | solution.py:406
  40.1 0.0 copy-done.3
  40.1 0.0 copy-done.1
  40.1 6.0 %first.1 = (bf16[32,256,256]{2,1,0:T(8,128)(2,1)S(1)}, bf16[32,256,256]{2,1,0:T(8,128)(2,1)S(1)}, f32[64,8,128]{2,1,0:T(8,128)S(1)}, f32[64,8,128]{2,1,0:T(8,128...) custom-call(f32[480,128]{1,0:T(8,128)S(1)} %bitcast.9, ...), custom_call_target="tpu_custom_call" | custom-call | tf_op jit(solution)/shard_map/first/pallas_call | solution.py:427
  46.1 4.9 %collective-permute-start.5 = (f32[8,128]{1,0:T(8,128)S(1)}, f32[8,128]{1,0:T(8,128)S(1)}, u32[]{:S(2)}, u32[]{:S(2)}) collective-permute-start(f32[8,128]{1,0:T(8,128)S(1)} %get-tuple-element.30.own_far), channel_id=1, source_target_pairs={{32,64},{64,32},{96,128},{128,96},{160,192},{192,160},{224,256},{2... | collective-permute-start | bytes 12296 | tf_op jit(solution)/shard_map/ppermute | solution.py:364
  51.1 2.0 %collective-permute-start.4 = (f32[8,128]{1,0:T(8,128)S(1)}, f32[8,128]{1,0:T(8,128)S(1)}, u32[]{:S(2)}, u32[]{:S(2)}) collective-permute-start(f32[8,128]{1,0:T(8,128)S(1)} %get-tuple-element.29.own_near), channel_id=1, source_target_pairs={{0,32},{32,0},{64,96},{96,64},{128,160},{160,128},{192,224},{224,1... | collective-permute-start | bytes 12296 | tf_op jit(solution)/shard_map/ppermute | solution.py:365
  53.0 0.7 %collective-permute-done.5.beside.far = f32[8,128]{1,0:T(8,128)S(1)} collective-permute-done((f32[8,128]{1,0:T(8,128)S(1)}, f32[8,128]{1,0:T(8,128)S(1)}, u32[]{:S(2)}, u32[]{:S(2)}) %collective-permute-start.5) | collective-permute-done | bytes 4128 | tf_op jit(solution)/shard_map/ppermute | solution.py:364
  53.7 0.1 columns.2
  53.8 2.8 %collective-permute-done.4.beside.near = f32[8,128]{1,0:T(8,128)S(1)} collective-permute-done((f32[8,128]{1,0:T(8,128)S(1)}, f32[8,128]{1,0:T(8,128)S(1)}, u32[]{:S(2)}, u32[]{:S(2)}) %collective-permute-start.4) | collective-permute-done | bytes 4128 | tf_op jit(solution)/shard_map/ppermute | solution.py:365
  56.6 0.1 columns.3
  56.7 0.0 collective-permute-start.6
  56.7 3.0 %collective-permute-start.7 = (f32[24,128]{1,0:T(8,128)S(1)}, f32[24,128]{1,0:T(8,128)S(1)}, u32[]{:S(2)}, u32[]{:S(2)}) collective-permute-start(f32[24,128]{1,0:T(8,128)S(1)} %get-tuple-element.36), channel_id=1, source_target_pairs={{1,0},{2,1},{3,2},{4,3},{5,4},{6,5},{7,6},{8,7},{9,8},{10,9},{11,1... | collective-permute-start | bytes 36872 | tf_op jit(solution)/shard_map/ppermute | solution.py:372
  59.6 1.4 %collective-permute-done.6.from_left = f32[24,128]{1,0:T(8,128)S(1)} collective-permute-done((f32[24,128]{1,0:T(8,128)S(1)}, f32[24,128]{1,0:T(8,128)S(1)}, u32[]{:S(2)}, u32[]{:S(2)}) %collective-permute-start.6) | collective-permute-done | bytes 12320 | tf_op jit(solution)/shard_map/ppermute | solution.py:371
  61.0 0.0 collective-permute-done.7.from_right
  61.0 3.8 %last.1 = f32[2048,128]{1,0:T(8,128)} custom-call(s32[8,128]{1,0:T(8,128)S(1)} %get-tuple-element.27.row_of, f32[2112,128]{1,0:T(8,128)S(1)} %get-tuple-element.28.partial, f32[2048,128]{1,0:T(8,128)S(1)} %bitcast.8, f32[512,128]{1,0:T(8,128)S(1)} %copy-done.3, f32[8,128]{1,0:T(8,128)S(1)} %collective-permute-done.4.beside.near, ...), custom_call_target="tpu_custom_call" | custom-call | tf_op jit(solution)/shard_map/last/pallas_call | solution.py:465
  (1 shorter events, 0.0 us)
Async XLA Ops:
  0.0 40.1 %copy-start.3 = (f32[512,128]{1,0:T(8,128)S(1)}, f32[512,128]{1,0:T(8,128)}, u32[]{:S(2)}) copy-start(f32[512,128]{1,0:T(8,128)} %flow.11) | copy-start | bytes 786436
  0.0 40.1 %copy-start.1 = (f32[4,512,128]{2,1,0:T(8,128)S(1)}, f32[4,512,128]{2,1,0:T(8,128)}, u32[]{:S(2)}) copy-start(f32[4,512,128]{2,1,0:T(8,128)} %param.10) | copy-start | bytes 3145732
  2.6 37.6 %all-to-all-start = ((f32[32,1,1920]{2,1,0:T(1,128)}), f32[32,1,1920]{2,1,0:T(1,128)S(1)}, u32[]{:S(2)}, u32[]{:S(2)}) async-start(f32[32,1,1920]{2,1,0:T(1,128)} %bitcast.10), calls=%async_computation | async-start | bytes 491520 | tf_op jit(solution)/shard_map/all_to_all | solution.py:406
  20.3 10.6 %collective-permute-start = (f32[8,128]{1,0:T(8,128)}, f32[8,128]{1,0:T(8,128)S(1)}, u32[]{:S(2)}, u32[]{:S(2)}) collective-permute-start(f32[8,128]{1,0:T(8,128)} %get-tuple-element.23), channel_id=1, source_target_pairs={{0,32},{32,0},{64,96},{96,64},{128,160},{160,128},{192,224},{224,1... | collective-permute-start | bytes 12296 | tf_op jit(solution)/shard_map/ppermute | solution.py:365
  23.7 7.8 %collective-permute-start.1 = (f32[8,128]{1,0:T(8,128)}, f32[8,128]{1,0:T(8,128)S(1)}, u32[]{:S(2)}, u32[]{:S(2)}) collective-permute-start(f32[8,128]{1,0:T(8,128)} %get-tuple-element.24), channel_id=1, source_target_pairs={{32,64},{64,32},{96,128},{128,96},{160,192},{192,160},{224,256},{2... | collective-permute-start | bytes 12296 | tf_op jit(solution)/shard_map/ppermute | solution.py:364
  27.9 4.5 %collective-permute-start.2 = (f32[8,128]{1,0:T(8,128)}, f32[8,128]{1,0:T(8,128)S(1)}, u32[]{:S(2)}, u32[]{:S(2)}) collective-permute-start(f32[8,128]{1,0:T(8,128)} %get-tuple-element.25), channel_id=1, source_target_pairs={{0,1},{1,2},{2,3},{3,4},{4,5},{5,6},{6,7},{7,8},{8,9},{9,10},{10,1... | collective-permute-start | bytes 12296 | tf_op jit(solution)/shard_map/ppermute | solution.py:371
  27.9 4.5 %collective-permute-start.3 = (f32[8,128]{1,0:T(8,128)}, f32[8,128]{1,0:T(8,128)S(1)}, u32[]{:S(2)}, u32[]{:S(2)}) collective-permute-start(f32[8,128]{1,0:T(8,128)} %get-tuple-element.26), channel_id=1, source_target_pairs={{1,0},{2,1},{3,2},{4,3},{5,4},{6,5},{7,6},{8,7},{9,8},{10,9},{11,1... | collective-permute-start | bytes 12296 | tf_op jit(solution)/shard_map/ppermute | solution.py:372
  32.4 1.2 %copy-start = (f32[4,512,128]{2,1,0:T(8,128)S(1)}, f32[4,512,128]{2,1,0:T(8,128)}, u32[]{:S(2)}) copy-start(f32[4,512,128]{2,1,0:T(8,128)} %param.10) | copy-start | bytes 3145732
  33.6 0.9 %copy-start.2 = (f32[512,128]{1,0:T(8,128)S(1)}, f32[512,128]{1,0:T(8,128)}, u32[]{:S(2)}) copy-start(f32[512,128]{1,0:T(8,128)} %flow.11) | copy-start | bytes 786436
  46.1 7.6 %collective-permute-start.5 = (f32[8,128]{1,0:T(8,128)S(1)}, f32[8,128]{1,0:T(8,128)S(1)}, u32[]{:S(2)}, u32[]{:S(2)}) collective-permute-start(f32[8,128]{1,0:T(8,128)S(1)} %get-tuple-element.30.own_far), channel_id=1, source_target_pairs={{32,64},{64,32},{96,128},{128,96},{160,192},{192,160},{224,256},{2... | collective-permute-start | bytes 12296 | tf_op jit(solution)/shard_map/ppermute | solution.py:364
  51.1 5.5 %collective-permute-start.4 = (f32[8,128]{1,0:T(8,128)S(1)}, f32[8,128]{1,0:T(8,128)S(1)}, u32[]{:S(2)}, u32[]{:S(2)}) collective-permute-start(f32[8,128]{1,0:T(8,128)S(1)} %get-tuple-element.29.own_near), channel_id=1, source_target_pairs={{0,32},{32,0},{64,96},{96,64},{128,160},{160,128},{192,224},{224,1... | collective-permute-start | bytes 12296 | tf_op jit(solution)/shard_map/ppermute | solution.py:365
  56.7 4.3 %collective-permute-start.6 = (f32[24,128]{1,0:T(8,128)S(1)}, f32[24,128]{1,0:T(8,128)S(1)}, u32[]{:S(2)}, u32[]{:S(2)}) collective-permute-start(f32[24,128]{1,0:T(8,128)S(1)} %get-tuple-element.35), channel_id=1, source_target_pairs={{0,1},{1,2},{2,3},{3,4},{4,5},{5,6},{6,7},{7,8},{8,9},{9,10},{10,1... | collective-permute-start | bytes 36872 | tf_op jit(solution)/shard_map/ppermute | solution.py:371
  56.7 4.4 %collective-permute-start.7 = (f32[24,128]{1,0:T(8,128)S(1)}, f32[24,128]{1,0:T(8,128)S(1)}, u32[]{:S(2)}, u32[]{:S(2)}) collective-permute-start(f32[24,128]{1,0:T(8,128)S(1)} %get-tuple-element.36), channel_id=1, source_target_pairs={{1,0},{2,1},{3,2},{4,3},{5,4},{6,5},{7,6},{8,7},{9,8},{10,9},{11,1... | collective-permute-start | bytes 36872 | tf_op jit(solution)/shard_map/ppermute | solution.py:372

commit v4 on v3

--- a/solution.py
+++ b/solution.py
@@ -50,10 +50,11 @@
     for t in range(tiles):
         latest[dest[t]] = t
     send[...] = jnp.zeros(send.shape, f32)
+    send[pl.ds(CAP * EACH, latest.shape[0], LINES), :] = jnp.ones((latest.shape[0], CELLS), f32)
     centre_of[...] = cell[...].astype(f32) + offset[...]
     factor_of[...] = (-0.5 / math.log(2.0)) / (width[...] * width[...])
     particle = lax.broadcasted_iota(jnp.int32, (tiles, CELLS), 0) * CELLS + lanes_of(tiles)
-    live_of[...] = jnp.where(particle < live[0], rate[...], 0.0)
+    live_of[...] = jnp.where(particle < live[0:1, 0:1], rate[...], 0.0)
     turn = lanes_of(1) % CAP
     for t in range(tiles):
         slot = (latest[dest[t]] == t).astype(jnp.int32)
@@ -173,18 +174,20 @@
         sums[2 * p + i] = part + pltpu.roll(part, 4, 0)
 
 
+def pair_sources(sums, turned_weights, goals, rates, scale, p):
+    nothing = jnp.zeros((8, CELLS), f32)
+    forces = [high_and_low(goals[t] - rates[t] * sums[t]) for t in (2 * p, 2 * p + 1)]
+    forces = jnp.concatenate(
+        [jnp.concatenate([forces[0], nothing], 1), jnp.concatenate([nothing, forces[1]], 1)], 0
+    ).astype(bf16)
+    both = jnp.dot(forces, turned_weights[p], preferred_element_type=f32)
+    both = scale * (both[:, :CELLS] + both[:, CELLS:])
+    return [both[8 * i : 8 * i + 4, :] + both[8 * i + 4 : 8 * i + 8, :] for i in range(2)]
+
+
 def add_sources(sums, turned_weights, goals, rates, row_of, out, first, scale):
-    nothing = jnp.zeros((8, CELLS), f32)
     for p in range(turned_weights.shape[0]):
-        forces = [high_and_low(goals[t] - rates[t] * sums[t]) for t in (2 * p, 2 * p + 1)]
-        forces = jnp.concatenate(
-            [jnp.concatenate([forces[0], nothing], 1), jnp.concatenate([nothing, forces[1]], 1)], 0
-        ).astype(bf16)
-        both = jnp.dot(forces, turned_weights[p], preferred_element_type=f32)
-        both = both[:, :CELLS] + both[:, CELLS:]
-        for i in range(2):
-            part = both[8 * i : 8 * i + 8, :]
-            part = scale * (part[0:4, :] + part[4:8, :])
+        for i, part in enumerate(pair_sources(sums, turned_weights, goals, rates, scale, p)):
             lines = pl.ds(row_of[0, 2 * p + i] + first, VARS, out.shape[0] // VARS)
             out[lines, :] = out[lines, :] + part
 
@@ -210,9 +213,19 @@
         rates[t] = jnp.broadcast_to(scaled * whole, (8, CELLS))
 
 
+def chunk_without_source(one, state, flow, r0):
+    rows = flow.shape[0]
+    change = chunk_rates(one, flow, None, r0, 0, 0)
+    chunk = []
+    for k in range(VARS):
+        now = one[at_row(k, r0, rows) : at_row(k, r0 + CHUNK, rows), :]
+        chunk.append(0.75 * state[k * rows + r0 : k * rows + r0 + CHUNK, :] + 0.25 * now + quarter * change[k])
+    return chunk
+
+
 def first_kernel(
-    got, waves, state, flow, weights, turned_weights, goals, rates, row_list, partial, near, far, right, left,
-    one, samples, sums, row_of, sem,
+    got, waves, state, flow, weights, turned_weights, goals, rates, row_list, one, samples, near, far,
+    ends, sums, row_of, sem,
 ):
     pairs = got.shape[0] // LINES
     slots = CAP * pairs
@@ -234,21 +247,36 @@
         see_pair(samples, weights, sums, p)
     add_sources(sums, turned_weights, goals, rates, row_of, one, TOP, time_step)
     sample(one, TOP, row_of, samples)
-    for p in range(slots // 2):
+    start, end = (chunk_without_source(one, state, flow, r0) for r0 in (0, rows - CHUNK))
+    ends[...] = jnp.concatenate([line[0:1, :] for line in start] + [line[CHUNK - 1 :, :] for line in end], 0)
+    for p in range(pairs):
+        at = [row_of[0, 2 * p + i] for i in range(2)]
+
+        @pl.when((at[0] == 0) | (at[0] == rows - 1) | (at[1] == 0) | (at[1] == rows - 1))
+        def _(p=p, at=at):
+            see_pair(samples, weights, sums, p)
+            for r, part in zip(at, pair_sources(sums, turned_weights, goals, rates, quarter, p)):
+                ends[0:4, :] = ends[0:4, :] + jnp.where(r == 0, part, 0.0)
+                ends[4:8, :] = ends[4:8, :] + jnp.where(r == rows - 1, part, 0.0)
+
+    messages = []
+    for r, start in ((0, 0), (rows - 1, 4)):
+        lines = [one[at_row(k, r, rows) : at_row(k, r, rows) + 1, :] for k in range(VARS)]
+        messages.append(jnp.concatenate(lines + [ends[start : start + 4, :]], 0))
+    near[...], far[...] = by_pair(messages[1], messages[0])
+
+
+def middle_kernel(
+    row_of, one, samples, state, flow, weights, turned_weights, goals, rates, partial, right, left, sums
+):
+    rows = flow.shape[0]
+    for p in range(weights.shape[0]):
         see_pair(samples, weights, sums, p)
     for r0 in range(0, rows, CHUNK):
-        change = chunk_rates(one, flow, None, r0, 0, 0)
-        for k in range(VARS):
-            here = slice(at_row(k, r0, rows), at_row(k, r0 + CHUNK, rows))
-            old = state[k * rows + r0 : k * rows + r0 + CHUNK, :]
-            partial[here, :] = 0.75 * old + 0.25 * one[here, :] + quarter * change[k]
+        for k, chunk in enumerate(chunk_without_source(one, state, flow, r0)):
+            partial[at_row(k, r0, rows) : at_row(k, r0 + CHUNK, rows), :] = chunk
     fill_rows(partial, [jnp.zeros((1, CELLS), f32)] * VARS, [jnp.zeros((1, CELLS), f32)] * VARS)
     add_sources(sums, turned_weights, goals, rates, row_of, partial, TOP, quarter)
-    ends = []
-    for r in (0, rows - 1):
-        starts = [at_row(k, r, rows) for k in range(VARS)]
-        ends.append(jnp.concatenate([cells[at : at + 1, :] for cells in (one, partial) for at in starts], 0))
-    near[...], far[...] = by_pair(ends[1], ends[0])
     columns = []
     for lane in (0, CELLS - 1):
         columns += edge_columns(one, TOP, lane) + edge_columns(partial, TOP, lane)
@@ -397,11 +425,11 @@
     send = pl.pallas_call(
         slots_kernel,
         out_shape=shape((sectors * LINES, CELLS)),
-        in_specs=[smem()] * 3 + [vmem()] * 5,
+        in_specs=[smem()] * 2 + [vmem()] * 6,
         out_specs=vmem(),
         scratch_shapes=[pltpu.VMEM((tiles, CELLS), f32)] * 3 + [pltpu.SMEM((sectors,), jnp.int32)],
         name="slots",
-    )(dest_owner[:, 0], gas_row, live_count, part_target, part_offset, part_width, part_rate, cell_index)
+    )(dest_owner[:, 0], gas_row, live_count.reshape(1, 1), part_target, part_offset, part_width, part_rate, cell_index)
     send = send.reshape(sectors, 1, LINES * CELLS)
     got = lax.all_to_all(send, "azim", split_axis=0, concat_axis=0, tiled=True).reshape(sectors * LINES, CELLS)
 
@@ -424,7 +452,7 @@
         name="waves",
     )(state, mean_flow, near_first, far_first, from_left, from_right)
 
-    weights, turned_weights, goals, rates, row_list, partial, own_near, own_far, own_right, own_left = pl.pallas_call(
+    weights, turned_weights, goals, rates, row_list, one, samples, own_near, own_far = pl.pallas_call(
         first_kernel,
         out_shape=[
             shape((pairs, 2 * CELLS, 2 * CELLS), bf16),
@@ -433,16 +461,14 @@
             shape((slots, 8, CELLS)),
             shape((8, CELLS), jnp.int32),
             shape(padded),
+            shape((slots * 8, CELLS)),
             edge,
             edge,
-            shape((24, CELLS)),
-            shape((24, CELLS)),
         ],
         in_specs=[vmem()] * 4,
-        out_specs=[vmem()] * 10,
+        out_specs=[vmem()] * 9,
         scratch_shapes=[
-            pltpu.VMEM(padded, f32),
-            pltpu.VMEM((slots * 8, CELLS), f32),
+            pltpu.VMEM((8, CELLS), f32),
             pltpu.VMEM((slots, 8, CELLS), f32),
             pltpu.SMEM((8, CELLS), jnp.int32),
             pltpu.SemaphoreType.DMA,
@@ -451,6 +477,15 @@
         name="first",
     )(got, waves, state, mean_flow)
     near, far = to_axial(own_near, own_far)
+    partial, own_right, own_left = pl.pallas_call(
+        middle_kernel,
+        out_shape=[shape(padded), shape((24, CELLS)), shape((24, CELLS))],
+        in_specs=[smem()] + [vmem()] * 8,
+        out_specs=[vmem()] * 3,
+        scratch_shapes=[pltpu.VMEM((slots, 8, CELLS), f32)],
+        compiler_params=room(15),
+        name="middle",
+    )(row_list, one, samples, state, mean_flow, weights, turned_weights, goals, rates)
     right, left = own_right, own_left
     for is_far, beside in ((True, far), (False, near)):
         right, left = pl.pallas_call(

time: 65.3 us -> 63.7 us (0.975)
  local copies, waits for them, and re-layouts: 2.18 us -> 0.01 us
  Pallas kernels: 14.9 us -> 16.1 us
    pallas_call x0 -> x1, Pallas kernels: none -> 2.63 us  [per_device(): pl.pallas_call(middle_kernel, out_shape=[shape(padded), shape((24, CELLS)...]
    unnamed x8 -> x4, local copies, waits for them, and re-layouts: 2.18 us -> 0.01 us
    all_to_all x1, waiting for transfers between devices: 4.66 us -> 6.83 us  [per_device(): lax.all_to_all(send, 'azim', split_axis=0, concat_axis=0, tiled=True)]
    ppermute x2, waiting for transfers between devices: 2.76 us -> 0.81 us  [to_axial(): return (lax.ppermute(near, 'axial', pairs(0)), far)]
    pallas_call x1, Pallas kernels: 5.99 us -> 4.42 us  [per_device(): pl.pallas_call(first_kernel, out_shape=[shape((pairs, 2 * CELLS, 2 * CELL...]
    ppermute x2, waiting for transfers between devices: 1.34 us -> 0.66 us  [to_axial(): far = lax.ppermute(far, 'axial', pairs(1))]
  transfers between devices with their start and end apart: 9 -> 9, of which waited for: 6 -> 5; matrix products, arithmetic and copies ran while one was open for 0% -> 0% of each run, Pallas kernels for 5% -> 9%
where the time goes in v4:
time: 63.7 us; the launch traced here: 63.3 us
  starting transfers between devices  35.9 us (56%)
  Pallas kernels  16.1 us (25%)
  waiting for transfers between devices  10.6 us (17%)
  between operations  0.74 us (1%)
    all_to_all x1, starting transfers between devices, per_device(): lax.all_to_all(send, 'azim', split_axis=0, concat_axis=0, tiled=True)  15.5 us
    ppermute x2, starting transfers between devices, to_axial(): far = lax.ppermute(far, 'axial', pairs(1))  9.15 us
    all_to_all x1, waiting for transfers between devices, per_device(): lax.all_to_all(send, 'azim', split_axis=0, concat_axis=0, tiled=True)  6.83 us
    ppermute x2, starting transfers between devices, to_azimuthal(): lax.ppermute(left, 'azim', [((i + 1) % count, i) for i in range(count)])  5.9 us
    ppermute x2, starting transfers between devices, to_axial(): return (lax.ppermute(near, 'axial', pairs(0)), far)  5.34 us
    pallas_call x1, Pallas kernels, per_device(): pl.pallas_call(first_kernel, out_shape=[shape((pairs, 2 * CELLS, 2 * CELL...  4.42 us
    pallas_call x1, Pallas kernels, per_device(): pl.pallas_call(last_kernel, out_shape=shape(state.shape), in_specs=[smem(...  3.84 us
    pallas_call x1, Pallas kernels, per_device(): pl.pallas_call(middle_kernel, out_shape=[shape(padded), shape((24, CELLS)...  2.63 us
  transfers between devices with their start and end apart: 9, of which 5 were waited for; matrix products, arithmetic and copies ran while one was open for 0% of the time, Pallas kernels for 9%

profile of v4, /device:TPU:24, one launch (start us, length us, event | category | flops | bytes accessed | tf_op | source)
XLA Modules:
  0.0 63.3 jit_solution(16181398097725439217)
XLA Ops:
  0.7 0.0 copy-start
  0.7 0.0 copy-start.1
  0.7 1.9 %slots.1 = f32[480,128]{1,0:T(8,128)} custom-call(s32[32]{0:T(128)} %bitcast.14, s32[32]{0:T(128)} %gas_row.1, s32[1,1]{1,0:T(1,128)} %bitcast.6.live, f32[32,4,128]{2,1,0:T(4,128)} %target.1, f32[32,128]{1,0:T(8,128)} %offset.1, f32[32,128]{1,0:T(8,128)} %width.1, f32[32,128]{1,0:T(8,128)} %rate.1, s32[32,128]{1,0:T(8,128)} %cell.1), custom_call_target="tpu_custom_call" | custom-call | tf_op jit(solution)/shard_map/slots/pallas_call | solution.py:425
  2.6 15.5 %all-to-all-start = ((f32[32,1,1920]{2,1,0:T(1,128)}), f32[32,1,1920]{2,1,0:T(1,128)S(1)}, u32[]{:S(2)}, u32[]{:S(2)}) async-start(f32[32,1,1920]{2,1,0:T(1,128)} %bitcast.13), calls=%async_computation | async-start | bytes 491520 | tf_op jit(solution)/shard_map/all_to_all | solution.py:434
  18.1 2.3 %edges.1 = (f32[8,128]{1,0:T(8,128)}, f32[8,128]{1,0:T(8,128)}, f32[8,128]{1,0:T(8,128)}, f32[8,128]{1,0:T(8,128)}) custom-call(f32[2048,128]{1,0:T(8,128)} %bitcast.7, f32[512,128]{1,0:T(8,128)} %flow.13), custom_call_target="tpu_custom_call" | custom-call | tf_op jit(solution)/shard_map/edges/pallas_call | solution.py:436
  20.4 3.4 %collective-permute-start = (f32[8,128]{1,0:T(8,128)}, f32[8,128]{1,0:T(8,128)S(1)}, u32[]{:S(2)}, u32[]{:S(2)}) collective-permute-start(f32[8,128]{1,0:T(8,128)} %get-tuple-element.25), channel_id=1, source_target_pairs={{0,32},{32,0},{64,96},{96,64},{128,160},{160,128},{192,224},{224,1... | collective-permute-start | bytes 12296 | tf_op jit(solution)/shard_map/ppermute | solution.py:393
  23.7 4.2 %collective-permute-start.1 = (f32[8,128]{1,0:T(8,128)}, f32[8,128]{1,0:T(8,128)S(1)}, u32[]{:S(2)}, u32[]{:S(2)}) collective-permute-start(f32[8,128]{1,0:T(8,128)} %get-tuple-element.26), channel_id=1, source_target_pairs={{32,64},{64,32},{96,128},{128,96},{160,192},{192,160},{224,256},{2... | collective-permute-start | bytes 12296 | tf_op jit(solution)/shard_map/ppermute | solution.py:392
  27.9 0.0 collective-permute-start.2
  28.0 2.9 %collective-permute-start.3 = (f32[8,128]{1,0:T(8,128)}, f32[8,128]{1,0:T(8,128)S(1)}, u32[]{:S(2)}, u32[]{:S(2)}) collective-permute-start(f32[8,128]{1,0:T(8,128)} %get-tuple-element.28), channel_id=1, source_target_pairs={{1,0},{2,1},{3,2},{4,3},{5,4},{6,5},{7,6},{8,7},{9,8},{10,9},{11,1... | collective-permute-start | bytes 12296 | tf_op jit(solution)/shard_map/ppermute | solution.py:400
  30.9 0.0 collective-permute-done.near.near_first
  30.9 0.7 %collective-permute-done.1.far.far_first = f32[8,128]{1,0:T(8,128)S(1)} collective-permute-done((f32[8,128]{1,0:T(8,128)}, f32[8,128]{1,0:T(8,128)S(1)}, u32[]{:S(2)}, u32[]{:S(2)}) %collective-permute-start.1) | collective-permute-done | bytes 4128 | tf_op jit(solution)/shard_map/ppermute | solution.py:392
  31.6 0.9 %collective-permute-done.2.from_left = f32[8,128]{1,0:T(8,128)S(1)} collective-permute-done((f32[8,128]{1,0:T(8,128)}, f32[8,128]{1,0:T(8,128)S(1)}, u32[]{:S(2)}, u32[]{:S(2)}) %collective-permute-start.2) | collective-permute-done | bytes 4128 | tf_op jit(solution)/shard_map/ppermute | solution.py:399
  32.4 0.0 collective-permute-done.3.from_right
  32.4 0.0 copy-done
  32.4 0.0 copy-done.1
  32.5 0.9 %waves.1 = f32[2112,128]{1,0:T(8,128)S(1)} custom-call(f32[2048,128]{1,0:T(8,128)S(1)} %bitcast.8, f32[512,128]{1,0:T(8,128)S(1)} %copy-done.1, f32[8,128]{1,0:T(8,128)S(1)} %collective-permute-done.near.near_first, f32[8,128]{1,0:T(8,128)S(1)} %collective-permute-done.1.far.far_first, f32[8,128]{1,0:T(8,128)S(1)} %collective-permute-done.2.from_left, ...), custom_call_target="tpu_custom_call" | custom-call | tf_op jit(solution)/shard_map/waves/pallas_call | solution.py:445
  33.3 6.8 %all-to-all-done = f32[32,1,1920]{2,1,0:T(1,128)S(1)} async-done(((f32[32,1,1920]{2,1,0:T(1,128)}), f32[32,1,1920]{2,1,0:T(1,128)S(1)}, u32[]{:S(2)}, u32[]{:S(2)}) %all-to-all-start) | async-done | bytes 245792 | tf_op jit(solution)/shard_map/all_to_all | solution.py:434
  40.1 4.4 %first.1 = (bf16[32,256,256]{2,1,0:T(8,128)(2,1)S(1)}, bf16[32,256,256]{2,1,0:T(8,128)(2,1)S(1)}, f32[64,8,128]{2,1,0:T(8,128)S(1)}, f32[64,8,128]{2,1,0:T(8,128...) custom-call(f32[480,128]{1,0:T(8,128)S(1)} %bitcast.12, ...), custom_call_target="tpu_custom_call" | custom-call | tf_op jit(solution)/shard_map/first/pallas_call | solution.py:455
  44.6 5.0 %collective-permute-start.5 = (f32[8,128]{1,0:T(8,128)S(1)}, f32[8,128]{1,0:T(8,128)S(1)}, u32[]{:S(2)}, u32[]{:S(2)}) collective-permute-start(f32[8,128]{1,0:T(8,128)S(1)} %get-tuple-element.38.own_far), channel_id=1, source_target_pairs={{32,64},{64,32},{96,128},{128,96},{160,192},{192,160},{224,256},{2... | collective-permute-start | bytes 12296 | tf_op jit(solution)/shard_map/ppermute | solution.py:392
  49.5 2.0 %collective-permute-start.4 = (f32[8,128]{1,0:T(8,128)S(1)}, f32[8,128]{1,0:T(8,128)S(1)}, u32[]{:S(2)}, u32[]{:S(2)}) collective-permute-start(f32[8,128]{1,0:T(8,128)S(1)} %get-tuple-element.37.own_near), channel_id=1, source_target_pairs={{0,32},{32,0},{64,96},{96,64},{128,160},{160,128},{192,224},{224,1... | collective-permute-start | bytes 12296 | tf_op jit(solution)/shard_map/ppermute | solution.py:393
  51.5 2.6 %middle.1 = (f32[2112,128]{1,0:T(8,128)S(1)}, f32[24,128]{1,0:T(8,128)S(1)}, f32[24,128]{1,0:T(8,128)S(1)}) custom-call(s32[8,128]{1,0:T(8,128)S(1)} %get-tuple-element.29.row_of, f32[2112,128]{1,0:T(8,128)S(1)} %get-tuple-element.30.one, f32[512,128]{1,0:T(8,128)S(1)} %get-tuple-element.31.samples, f32[2048,128]{1,0:T(8,128)S(1)} %bitcast.10, ...), custom_call_target="tpu_custom_call" | custom-call | tf_op jit(solution)/shard_map/middle/pallas_call | solution.py:480
  54.1 0.0 collective-permute-done.5.beside.far
  54.1 0.1 columns.2
  54.2 0.8 %collective-permute-done.4.beside.near = f32[8,128]{1,0:T(8,128)S(1)} collective-permute-done((f32[8,128]{1,0:T(8,128)S(1)}, f32[8,128]{1,0:T(8,128)S(1)}, u32[]{:S(2)}, u32[]{:S(2)}) %collective-permute-start.4) | collective-permute-done | bytes 4128 | tf_op jit(solution)/shard_map/ppermute | solution.py:393
  55.1 0.1 columns.3
  55.1 0.0 collective-permute-start.6
  55.1 3.0 %collective-permute-start.7 = (f32[24,128]{1,0:T(8,128)S(1)}, f32[24,128]{1,0:T(8,128)S(1)}, u32[]{:S(2)}, u32[]{:S(2)}) collective-permute-start(f32[24,128]{1,0:T(8,128)S(1)} %get-tuple-element.44), channel_id=1, source_target_pairs={{1,0},{2,1},{3,2},{4,3},{5,4},{6,5},{7,6},{8,7},{9,8},{10,9},{11,1... | collective-permute-start | bytes 36872 | tf_op jit(solution)/shard_map/ppermute | solution.py:400
  58.1 1.4 %collective-permute-done.6.from_left = f32[24,128]{1,0:T(8,128)S(1)} collective-permute-done((f32[24,128]{1,0:T(8,128)S(1)}, f32[24,128]{1,0:T(8,128)S(1)}, u32[]{:S(2)}, u32[]{:S(2)}) %collective-permute-start.6) | collective-permute-done | bytes 12320 | tf_op jit(solution)/shard_map/ppermute | solution.py:399
  59.5 0.0 collective-permute-done.7.from_right
  59.5 3.8 %last.1 = f32[2048,128]{1,0:T(8,128)} custom-call(s32[8,128]{1,0:T(8,128)S(1)} %get-tuple-element.29.row_of, f32[2112,128]{1,0:T(8,128)S(1)} %get-tuple-element.36.partial, f32[2048,128]{1,0:T(8,128)S(1)} %bitcast.11, f32[512,128]{1,0:T(8,128)S(1)} %copy-done.1, f32[8,128]{1,0:T(8,128)S(1)} %collective-permute-done.4.beside.near, ...), custom_call_target="tpu_custom_call" | custom-call | tf_op jit(solution)/shard_map/last/pallas_call | solution.py:500
Async XLA Ops:
  0.7 31.8 %copy-start = (f32[4,512,128]{2,1,0:T(8,128)S(1)}, f32[4,512,128]{2,1,0:T(8,128)}, u32[]{:S(2)}) copy-start(f32[4,512,128]{2,1,0:T(8,128)} %param.10) | copy-start | bytes 3145732
  0.7 31.8 %copy-start.1 = (f32[512,128]{1,0:T(8,128)S(1)}, f32[512,128]{1,0:T(8,128)}, u32[]{:S(2)}) copy-start(f32[512,128]{1,0:T(8,128)} %flow.13) | copy-start | bytes 786436
  2.6 37.6 %all-to-all-start = ((f32[32,1,1920]{2,1,0:T(1,128)}), f32[32,1,1920]{2,1,0:T(1,128)S(1)}, u32[]{:S(2)}, u32[]{:S(2)}) async-start(f32[32,1,1920]{2,1,0:T(1,128)} %bitcast.13), calls=%async_computation | async-start | bytes 491520 | tf_op jit(solution)/shard_map/all_to_all | solution.py:434
  20.4 10.6 %collective-permute-start = (f32[8,128]{1,0:T(8,128)}, f32[8,128]{1,0:T(8,128)S(1)}, u32[]{:S(2)}, u32[]{:S(2)}) collective-permute-start(f32[8,128]{1,0:T(8,128)} %get-tuple-element.25), channel_id=1, source_target_pairs={{0,32},{32,0},{64,96},{96,64},{128,160},{160,128},{192,224},{224,1... | collective-permute-start | bytes 12296 | tf_op jit(solution)/shard_map/ppermute | solution.py:393
  23.7 7.8 %collective-permute-start.1 = (f32[8,128]{1,0:T(8,128)}, f32[8,128]{1,0:T(8,128)S(1)}, u32[]{:S(2)}, u32[]{:S(2)}) collective-permute-start(f32[8,128]{1,0:T(8,128)} %get-tuple-element.26), channel_id=1, source_target_pairs={{32,64},{64,32},{96,128},{128,96},{160,192},{192,160},{224,256},{2... | collective-permute-start | bytes 12296 | tf_op jit(solution)/shard_map/ppermute | solution.py:392
  27.9 4.5 %collective-permute-start.2 = (f32[8,128]{1,0:T(8,128)}, f32[8,128]{1,0:T(8,128)S(1)}, u32[]{:S(2)}, u32[]{:S(2)}) collective-permute-start(f32[8,128]{1,0:T(8,128)} %get-tuple-element.27), channel_id=1, source_target_pairs={{0,1},{1,2},{2,3},{3,4},{4,5},{5,6},{6,7},{7,8},{8,9},{9,10},{10,1... | collective-permute-start | bytes 12296 | tf_op jit(solution)/shard_map/ppermute | solution.py:399
  28.0 4.5 %collective-permute-start.3 = (f32[8,128]{1,0:T(8,128)}, f32[8,128]{1,0:T(8,128)S(1)}, u32[]{:S(2)}, u32[]{:S(2)}) collective-permute-start(f32[8,128]{1,0:T(8,128)} %get-tuple-element.28), channel_id=1, source_target_pairs={{1,0},{2,1},{3,2},{4,3},{5,4},{6,5},{7,6},{8,7},{9,8},{10,9},{11,1... | collective-permute-start | bytes 12296 | tf_op jit(solution)/shard_map/ppermute | solution.py:400
  44.6 9.6 %collective-permute-start.5 = (f32[8,128]{1,0:T(8,128)S(1)}, f32[8,128]{1,0:T(8,128)S(1)}, u32[]{:S(2)}, u32[]{:S(2)}) collective-permute-start(f32[8,128]{1,0:T(8,128)S(1)} %get-tuple-element.38.own_far), channel_id=1, source_target_pairs={{32,64},{64,32},{96,128},{128,96},{160,192},{192,160},{224,256},{2... | collective-permute-start | bytes 12296 | tf_op jit(solution)/shard_map/ppermute | solution.py:392
  49.5 5.5 %collective-permute-start.4 = (f32[8,128]{1,0:T(8,128)S(1)}, f32[8,128]{1,0:T(8,128)S(1)}, u32[]{:S(2)}, u32[]{:S(2)}) collective-permute-start(f32[8,128]{1,0:T(8,128)S(1)} %get-tuple-element.37.own_near), channel_id=1, source_target_pairs={{0,32},{32,0},{64,96},{96,64},{128,160},{160,128},{192,224},{224,1... | collective-permute-start | bytes 12296 | tf_op jit(solution)/shard_map/ppermute | solution.py:393
  55.1 4.3 %collective-permute-start.6 = (f32[24,128]{1,0:T(8,128)S(1)}, f32[24,128]{1,0:T(8,128)S(1)}, u32[]{:S(2)}, u32[]{:S(2)}) collective-permute-start(f32[24,128]{1,0:T(8,128)S(1)} %get-tuple-element.43), channel_id=1, source_target_pairs={{0,1},{1,2},{2,3},{3,4},{4,5},{5,6},{6,7},{7,8},{8,9},{9,10},{10,1... | collective-permute-start | bytes 36872 | tf_op jit(solution)/shard_map/ppermute | solution.py:399
  55.1 4.4 %collective-permute-start.7 = (f32[24,128]{1,0:T(8,128)S(1)}, f32[24,128]{1,0:T(8,128)S(1)}, u32[]{:S(2)}, u32[]{:S(2)}) collective-permute-start(f32[24,128]{1,0:T(8,128)S(1)} %get-tuple-element.44), channel_id=1, source_target_pairs={{1,0},{2,1},{3,2},{4,3},{5,4},{6,5},{7,6},{8,7},{9,8},{10,9},{11,1... | collective-permute-start | bytes 36872 | tf_op jit(solution)/shard_map/ppermute | solution.py:400

commit v5 on v4

--- a/solution.py
+++ b/solution.py
@@ -249,15 +249,20 @@
     sample(one, TOP, row_of, samples)
     start, end = (chunk_without_source(one, state, flow, r0) for r0 in (0, rows - CHUNK))
     ends[...] = jnp.concatenate([line[0:1, :] for line in start] + [line[CHUNK - 1 :, :] for line in end], 0)
-    for p in range(pairs):
-        at = [row_of[0, 2 * p + i] for i in range(2)]
-
-        @pl.when((at[0] == 0) | (at[0] == rows - 1) | (at[1] == 0) | (at[1] == rows - 1))
-        def _(p=p, at=at):
-            see_pair(samples, weights, sums, p)
-            for r, part in zip(at, pair_sources(sums, turned_weights, goals, rates, quarter, p)):
-                ends[0:4, :] = ends[0:4, :] + jnp.where(r == 0, part, 0.0)
-                ends[4:8, :] = ends[4:8, :] + jnp.where(r == rows - 1, part, 0.0)
+    places = [row_of[0, t] for t in range(slots)]
+    outer = [((r == 0) | (r == rows - 1)).astype(jnp.int32) for r in places]
+
+    @pl.when(functools.reduce(jnp.add, outer) > 0)
+    def _():
+        for p in range(pairs):
+
+            @pl.when(outer[2 * p] + outer[2 * p + 1] > 0)
+            def _(p=p):
+                see_pair(samples, weights, sums, p)
+                for i, part in enumerate(pair_sources(sums, turned_weights, goals, rates, quarter, p)):
+                    r = row_of[0, 2 * p + i]
+                    ends[0:4, :] = ends[0:4, :] + jnp.where(r == 0, part, 0.0)
+                    ends[4:8, :] = ends[4:8, :] + jnp.where(r == rows - 1, part, 0.0)
 
     messages = []
     for r, start in ((0, 0), (rows - 1, 4)):

time: 63.7 us -> 63.4 us (level)
  no operation moved by 1% of the time
where the time goes in v5:
time: 63.4 us; the launch traced here: 63.1 us
  starting transfers between devices  35.9 us (57%)
  Pallas kernels  15.9 us (25%)
  waiting for transfers between devices  10.6 us (17%)
  between operations  0.74 us (1%)
    all_to_all x1, starting transfers between devices, per_device(): lax.all_to_all(send, 'azim', split_axis=0, concat_axis=0, tiled=True)  15.5 us
    ppermute x2, starting transfers between devices, to_axial(): far = lax.ppermute(far, 'axial', pairs(1))  9.14 us
    all_to_all x1, waiting for transfers between devices, per_device(): lax.all_to_all(send, 'azim', split_axis=0, concat_axis=0, tiled=True)  6.83 us
    ppermute x2, starting transfers between devices, to_azimuthal(): lax.ppermute(left, 'azim', [((i + 1) % count, i) for i in range(count)])  5.9 us
    ppermute x2, starting transfers between devices, to_axial(): return (lax.ppermute(near, 'axial', pairs(0)), far)  5.35 us
    pallas_call x1, Pallas kernels, per_device(): pl.pallas_call(first_kernel, out_shape=[shape((pairs, 2 * CELLS, 2 * CELL...  4.15 us
    pallas_call x1, Pallas kernels, per_device(): pl.pallas_call(last_kernel, out_shape=shape(state.shape), in_specs=[smem(...  3.84 us
    pallas_call x1, Pallas kernels, per_device(): pl.pallas_call(middle_kernel, out_shape=[shape(padded), shape((24, CELLS)...  2.64 us
  transfers between devices with their start and end apart: 9, of which 5 were waited for; matrix products, arithmetic and copies ran while one was open for 0% of the time, Pallas kernels for 9%

profile of v5, /device:TPU:24, one launch (start us, length us, event | category | flops | bytes accessed | tf_op | source)
XLA Modules:
  0.0 63.1 jit_solution(6632177748201617031)
XLA Ops:
  0.7 0.0 copy-start
  0.7 0.0 copy-start.1
  0.7 1.9 %slots.1 = f32[480,128]{1,0:T(8,128)} custom-call(s32[32]{0:T(128)} %bitcast.14, s32[32]{0:T(128)} %gas_row.1, s32[1,1]{1,0:T(1,128)} %bitcast.6.live, f32[32,4,128]{2,1,0:T(4,128)} %target.1, f32[32,128]{1,0:T(8,128)} %offset.1, f32[32,128]{1,0:T(8,128)} %width.1, f32[32,128]{1,0:T(8,128)} %rate.1, s32[32,128]{1,0:T(8,128)} %cell.1), custom_call_target="tpu_custom_call" | custom-call | tf_op jit(solution)/shard_map/slots/pallas_call | solution.py:430
  2.6 15.5 %all-to-all-start = ((f32[32,1,1920]{2,1,0:T(1,128)}), f32[32,1,1920]{2,1,0:T(1,128)S(1)}, u32[]{:S(2)}, u32[]{:S(2)}) async-start(f32[32,1,1920]{2,1,0:T(1,128)} %bitcast.13), calls=%async_computation | async-start | bytes 491520 | tf_op jit(solution)/shard_map/all_to_all | solution.py:439
  18.1 2.3 %edges.1 = (f32[8,128]{1,0:T(8,128)}, f32[8,128]{1,0:T(8,128)}, f32[8,128]{1,0:T(8,128)}, f32[8,128]{1,0:T(8,128)}) custom-call(f32[2048,128]{1,0:T(8,128)} %bitcast.7, f32[512,128]{1,0:T(8,128)} %flow.13), custom_call_target="tpu_custom_call" | custom-call | tf_op jit(solution)/shard_map/edges/pallas_call | solution.py:441
  20.4 3.4 %collective-permute-start = (f32[8,128]{1,0:T(8,128)}, f32[8,128]{1,0:T(8,128)S(1)}, u32[]{:S(2)}, u32[]{:S(2)}) collective-permute-start(f32[8,128]{1,0:T(8,128)} %get-tuple-element.25), channel_id=1, source_target_pairs={{0,32},{32,0},{64,96},{96,64},{128,160},{160,128},{192,224},{224,1... | collective-permute-start | bytes 12296 | tf_op jit(solution)/shard_map/ppermute | solution.py:398
  23.7 4.2 %collective-permute-start.1 = (f32[8,128]{1,0:T(8,128)}, f32[8,128]{1,0:T(8,128)S(1)}, u32[]{:S(2)}, u32[]{:S(2)}) collective-permute-start(f32[8,128]{1,0:T(8,128)} %get-tuple-element.26), channel_id=1, source_target_pairs={{32,64},{64,32},{96,128},{128,96},{160,192},{192,160},{224,256},{2... | collective-permute-start | bytes 12296 | tf_op jit(solution)/shard_map/ppermute | solution.py:397
  27.9 0.0 collective-permute-start.2
  28.0 2.9 %collective-permute-start.3 = (f32[8,128]{1,0:T(8,128)}, f32[8,128]{1,0:T(8,128)S(1)}, u32[]{:S(2)}, u32[]{:S(2)}) collective-permute-start(f32[8,128]{1,0:T(8,128)} %get-tuple-element.28), channel_id=1, source_target_pairs={{1,0},{2,1},{3,2},{4,3},{5,4},{6,5},{7,6},{8,7},{9,8},{10,9},{11,1... | collective-permute-start | bytes 12296 | tf_op jit(solution)/shard_map/ppermute | solution.py:405
  30.9 0.0 collective-permute-done.near.near_first
  30.9 0.7 %collective-permute-done.1.far.far_first = f32[8,128]{1,0:T(8,128)S(1)} collective-permute-done((f32[8,128]{1,0:T(8,128)}, f32[8,128]{1,0:T(8,128)S(1)}, u32[]{:S(2)}, u32[]{:S(2)}) %collective-permute-start.1) | collective-permute-done | bytes 4128 | tf_op jit(solution)/shard_map/ppermute | solution.py:397
  31.6 0.9 %collective-permute-done.2.from_left = f32[8,128]{1,0:T(8,128)S(1)} collective-permute-done((f32[8,128]{1,0:T(8,128)}, f32[8,128]{1,0:T(8,128)S(1)}, u32[]{:S(2)}, u32[]{:S(2)}) %collective-permute-start.2) | collective-permute-done | bytes 4128 | tf_op jit(solution)/shard_map/ppermute | solution.py:404
  32.4 0.0 collective-permute-done.3.from_right
  32.4 0.0 copy-done
  32.4 0.0 copy-done.1
  32.5 0.9 %waves.1 = f32[2112,128]{1,0:T(8,128)S(1)} custom-call(f32[2048,128]{1,0:T(8,128)S(1)} %bitcast.8, f32[512,128]{1,0:T(8,128)S(1)} %copy-done.1, f32[8,128]{1,0:T(8,128)S(1)} %collective-permute-done.near.near_first, f32[8,128]{1,0:T(8,128)S(1)} %collective-permute-done.1.far.far_first, f32[8,128]{1,0:T(8,128)S(1)} %collective-permute-done.2.from_left, ...), custom_call_target="tpu_custom_call" | custom-call | tf_op jit(solution)/shard_map/waves/pallas_call | solution.py:450
  33.3 6.8 %all-to-all-done = f32[32,1,1920]{2,1,0:T(1,128)S(1)} async-done(((f32[32,1,1920]{2,1,0:T(1,128)}), f32[32,1,1920]{2,1,0:T(1,128)S(1)}, u32[]{:S(2)}, u32[]{:S(2)}) %all-to-all-start) | async-done | bytes 245792 | tf_op jit(solution)/shard_map/all_to_all | solution.py:439
  40.1 4.1 %first.1 = (bf16[32,256,256]{2,1,0:T(8,128)(2,1)S(1)}, bf16[32,256,256]{2,1,0:T(8,128)(2,1)S(1)}, f32[64,8,128]{2,1,0:T(8,128)S(1)}, f32[64,8,128]{2,1,0:T(8,128...) custom-call(f32[480,128]{1,0:T(8,128)S(1)} %bitcast.12, ...), custom_call_target="tpu_custom_call" | custom-call | tf_op jit(solution)/shard_map/first/pallas_call | solution.py:460
  44.3 5.0 %collective-permute-start.5 = (f32[8,128]{1,0:T(8,128)S(1)}, f32[8,128]{1,0:T(8,128)S(1)}, u32[]{:S(2)}, u32[]{:S(2)}) collective-permute-start(f32[8,128]{1,0:T(8,128)S(1)} %get-tuple-element.38.own_far), channel_id=1, source_target_pairs={{32,64},{64,32},{96,128},{128,96},{160,192},{192,160},{224,256},{2... | collective-permute-start | bytes 12296 | tf_op jit(solution)/shard_map/ppermute | solution.py:397
  49.3 2.0 %collective-permute-start.4 = (f32[8,128]{1,0:T(8,128)S(1)}, f32[8,128]{1,0:T(8,128)S(1)}, u32[]{:S(2)}, u32[]{:S(2)}) collective-permute-start(f32[8,128]{1,0:T(8,128)S(1)} %get-tuple-element.37.own_near), channel_id=1, source_target_pairs={{0,32},{32,0},{64,96},{96,64},{128,160},{160,128},{192,224},{224,1... | collective-permute-start | bytes 12296 | tf_op jit(solution)/shard_map/ppermute | solution.py:398
  51.2 2.6 %middle.1 = (f32[2112,128]{1,0:T(8,128)S(1)}, f32[24,128]{1,0:T(8,128)S(1)}, f32[24,128]{1,0:T(8,128)S(1)}) custom-call(s32[8,128]{1,0:T(8,128)S(1)} %get-tuple-element.29.row_of, f32[2112,128]{1,0:T(8,128)S(1)} %get-tuple-element.30.one, f32[512,128]{1,0:T(8,128)S(1)} %get-tuple-element.31.samples, f32[2048,128]{1,0:T(8,128)S(1)} %bitcast.10, ...), custom_call_target="tpu_custom_call" | custom-call | tf_op jit(solution)/shard_map/middle/pallas_call | solution.py:485
  53.9 0.0 collective-permute-done.5.beside.far
  53.9 0.1 columns.2
  54.0 0.8 %collective-permute-done.4.beside.near = f32[8,128]{1,0:T(8,128)S(1)} collective-permute-done((f32[8,128]{1,0:T(8,128)S(1)}, f32[8,128]{1,0:T(8,128)S(1)}, u32[]{:S(2)}, u32[]{:S(2)}) %collective-permute-start.4) | collective-permute-done | bytes 4128 | tf_op jit(solution)/shard_map/ppermute | solution.py:398
  54.8 0.1 columns.3
  54.9 0.0 collective-permute-start.6
  54.9 3.0 %collective-permute-start.7 = (f32[24,128]{1,0:T(8,128)S(1)}, f32[24,128]{1,0:T(8,128)S(1)}, u32[]{:S(2)}, u32[]{:S(2)}) collective-permute-start(f32[24,128]{1,0:T(8,128)S(1)} %get-tuple-element.44), channel_id=1, source_target_pairs={{1,0},{2,1},{3,2},{4,3},{5,4},{6,5},{7,6},{8,7},{9,8},{10,9},{11,1... | collective-permute-start | bytes 36872 | tf_op jit(solution)/shard_map/ppermute | solution.py:405
  57.8 1.4 %collective-permute-done.6.from_left = f32[24,128]{1,0:T(8,128)S(1)} collective-permute-done((f32[24,128]{1,0:T(8,128)S(1)}, f32[24,128]{1,0:T(8,128)S(1)}, u32[]{:S(2)}, u32[]{:S(2)}) %collective-permute-start.6) | collective-permute-done | bytes 12320 | tf_op jit(solution)/shard_map/ppermute | solution.py:404
  59.2 0.0 collective-permute-done.7.from_right
  59.2 3.8 %last.1 = f32[2048,128]{1,0:T(8,128)} custom-call(s32[8,128]{1,0:T(8,128)S(1)} %get-tuple-element.29.row_of, f32[2112,128]{1,0:T(8,128)S(1)} %get-tuple-element.36.partial, f32[2048,128]{1,0:T(8,128)S(1)} %bitcast.11, f32[512,128]{1,0:T(8,128)S(1)} %copy-done.1, f32[8,128]{1,0:T(8,128)S(1)} %collective-permute-done.4.beside.near, ...), custom_call_target="tpu_custom_call" | custom-call | tf_op jit(solution)/shard_map/last/pallas_call | solution.py:505
Async XLA Ops:
  0.7 31.8 %copy-start = (f32[4,512,128]{2,1,0:T(8,128)S(1)}, f32[4,512,128]{2,1,0:T(8,128)}, u32[]{:S(2)}) copy-start(f32[4,512,128]{2,1,0:T(8,128)} %param.10) | copy-start | bytes 3145732
  0.7 31.8 %copy-start.1 = (f32[512,128]{1,0:T(8,128)S(1)}, f32[512,128]{1,0:T(8,128)}, u32[]{:S(2)}) copy-start(f32[512,128]{1,0:T(8,128)} %flow.13) | copy-start | bytes 786436
  2.6 37.6 %all-to-all-start = ((f32[32,1,1920]{2,1,0:T(1,128)}), f32[32,1,1920]{2,1,0:T(1,128)S(1)}, u32[]{:S(2)}, u32[]{:S(2)}) async-start(f32[32,1,1920]{2,1,0:T(1,128)} %bitcast.13), calls=%async_computation | async-start | bytes 491520 | tf_op jit(solution)/shard_map/all_to_all | solution.py:439
  20.4 10.6 %collective-permute-start = (f32[8,128]{1,0:T(8,128)}, f32[8,128]{1,0:T(8,128)S(1)}, u32[]{:S(2)}, u32[]{:S(2)}) collective-permute-start(f32[8,128]{1,0:T(8,128)} %get-tuple-element.25), channel_id=1, source_target_pairs={{0,32},{32,0},{64,96},{96,64},{128,160},{160,128},{192,224},{224,1... | collective-permute-start | bytes 12296 | tf_op jit(solution)/shard_map/ppermute | solution.py:398
  23.7 7.8 %collective-permute-start.1 = (f32[8,128]{1,0:T(8,128)}, f32[8,128]{1,0:T(8,128)S(1)}, u32[]{:S(2)}, u32[]{:S(2)}) collective-permute-start(f32[8,128]{1,0:T(8,128)} %get-tuple-element.26), channel_id=1, source_target_pairs={{32,64},{64,32},{96,128},{128,96},{160,192},{192,160},{224,256},{2... | collective-permute-start | bytes 12296 | tf_op jit(solution)/shard_map/ppermute | solution.py:397
  27.9 4.5 %collective-permute-start.2 = (f32[8,128]{1,0:T(8,128)}, f32[8,128]{1,0:T(8,128)S(1)}, u32[]{:S(2)}, u32[]{:S(2)}) collective-permute-start(f32[8,128]{1,0:T(8,128)} %get-tuple-element.27), channel_id=1, source_target_pairs={{0,1},{1,2},{2,3},{3,4},{4,5},{5,6},{6,7},{7,8},{8,9},{9,10},{10,1... | collective-permute-start | bytes 12296 | tf_op jit(solution)/shard_map/ppermute | solution.py:404
  28.0 4.5 %collective-permute-start.3 = (f32[8,128]{1,0:T(8,128)}, f32[8,128]{1,0:T(8,128)S(1)}, u32[]{:S(2)}, u32[]{:S(2)}) collective-permute-start(f32[8,128]{1,0:T(8,128)} %get-tuple-element.28), channel_id=1, source_target_pairs={{1,0},{2,1},{3,2},{4,3},{5,4},{6,5},{7,6},{8,7},{9,8},{10,9},{11,1... | collective-permute-start | bytes 12296 | tf_op jit(solution)/shard_map/ppermute | solution.py:405
  44.3 9.6 %collective-permute-start.5 = (f32[8,128]{1,0:T(8,128)S(1)}, f32[8,128]{1,0:T(8,128)S(1)}, u32[]{:S(2)}, u32[]{:S(2)}) collective-permute-start(f32[8,128]{1,0:T(8,128)S(1)} %get-tuple-element.38.own_far), channel_id=1, source_target_pairs={{32,64},{64,32},{96,128},{128,96},{160,192},{192,160},{224,256},{2... | collective-permute-start | bytes 12296 | tf_op jit(solution)/shard_map/ppermute | solution.py:397
  49.3 5.5 %collective-permute-start.4 = (f32[8,128]{1,0:T(8,128)S(1)}, f32[8,128]{1,0:T(8,128)S(1)}, u32[]{:S(2)}, u32[]{:S(2)}) collective-permute-start(f32[8,128]{1,0:T(8,128)S(1)} %get-tuple-element.37.own_near), channel_id=1, source_target_pairs={{0,32},{32,0},{64,96},{96,64},{128,160},{160,128},{192,224},{224,1... | collective-permute-start | bytes 12296 | tf_op jit(solution)/shard_map/ppermute | solution.py:398
  54.9 4.3 %collective-permute-start.6 = (f32[24,128]{1,0:T(8,128)S(1)}, f32[24,128]{1,0:T(8,128)S(1)}, u32[]{:S(2)}, u32[]{:S(2)}) collective-permute-start(f32[24,128]{1,0:T(8,128)S(1)} %get-tuple-element.43), channel_id=1, source_target_pairs={{0,1},{1,2},{2,3},{3,4},{4,5},{5,6},{6,7},{7,8},{8,9},{9,10},{10,1... | collective-permute-start | bytes 36872 | tf_op jit(solution)/shard_map/ppermute | solution.py:404
  54.9 4.4 %collective-permute-start.7 = (f32[24,128]{1,0:T(8,128)S(1)}, f32[24,128]{1,0:T(8,128)S(1)}, u32[]{:S(2)}, u32[]{:S(2)}) collective-permute-start(f32[24,128]{1,0:T(8,128)S(1)} %get-tuple-element.44), channel_id=1, source_target_pairs={{1,0},{2,1},{3,2},{4,3},{5,4},{6,5},{7,6},{8,7},{9,8},{10,9},{11,1... | collective-permute-start | bytes 36872 | tf_op jit(solution)/shard_map/ppermute | solution.py:405
